TPU v7x, 512 devices: a whole 4x8x8 slice. The times are simulated.
512 devices in a mesh: dp: 64 (over z_hi, y, core), mp: 8 (over z_lo, x).
Axes of the slice: x: 4, y: 8, z: 8 (z_hi: 4, z_lo: 2; z = z_hi * 2 + z_lo), core: 2. Of those that a mesh axis runs over, the one named last changes fastest.
Arguments:
- hidden: bfloat16 [40960, 14336], P('dp', 'mp'), may hold values from -6 to 6
- out_grad: bfloat16 [40960, 512], P('dp'), may hold values from -0.23632812 to 0.23632812
- master: float32 [14336, 512], P(('mp', 'dp')), may hold values from -0.03 to 0.03
- moment_one: float32 [14336, 512], P(('mp', 'dp')), may hold values from -0.12 to 0.12
- moment_two: float32 [14336, 512], P(('mp', 'dp')), may hold values from 0.0001 to 0.001
- sign_flips: int32 [512], replicated, may hold values from -1 to 1, as said below
- step_count: int32 [1], replicated, may hold values from 1 to 8
Outputs:
- weights: bfloat16 [14336, 512], P('mp')
- update: float32 [14336, 512], P(('mp', 'dp'))
Inputs may be any that keep to these rules, and one draw needn't show every extreme that they name: `sign_flips`: each entry is -1 or 1.
All inputs are finite; a program needn't handle non-finite values.
Results may differ from a plain program's by a relative error of at most 0.007.
Values may be sent and summed in bfloat16 or wider, within the bound.
No kernel may reach another device: no remote copies, remote signals or barrier semaphores. Data moves between devices by JAX's collectives and lax.ppermute only.
A program may use at most 64 MiB of HBM per device.

v0:
```python
import jax
import jax.numpy as jnp
from jax import lax
from jax.sharding import PartitionSpec as P


def hadamard_table(order):
    table = jnp.ones((1, 1), jnp.float32)
    while table.shape[0] < order:
        table = jnp.concatenate(
            [jnp.concatenate([table, table], axis=1), jnp.concatenate([table, -table], axis=1)],
            axis=0,
        )
    return table


def local(hidden, out_grad, master, moment_one, moment_two, sign_flips, step_count):
    columns = out_grad.shape[1]
    factor = columns ** (-0.5)
    table = hadamard_table(columns) * factor
    table_half = table.astype(jnp.bfloat16)
    flips_half = sign_flips.astype(jnp.bfloat16)
    flips_full = sign_flips.astype(jnp.float32)
    replicas = lax.axis_size("dp")
    partial_value = lax.dot_general(
        hidden, out_grad, (((0,), (0,)), ((), ())), preferred_element_type=jnp.float32
    )
    signed = partial_value.astype(jnp.bfloat16) * flips_half[None, :]
    rotated = jnp.dot(signed, table_half, preferred_element_type=jnp.float32).astype(jnp.bfloat16)
    summed = lax.psum_scatter(rotated.astype(jnp.float32), "dp", scatter_dimension=0, tiled=True)
    gradient = summed / replicas
    steps_done = step_count[0].astype(jnp.float32)
    first = 0.9 * moment_one + 0.1 * gradient
    second = 0.95 * moment_two + 0.05 * gradient * gradient
    first_hat = first / (1.0 - jnp.power(jnp.float32(0.9), steps_done))
    second_hat = second / (1.0 - jnp.power(jnp.float32(0.95), steps_done))
    direction = first_hat / (jnp.sqrt(second_hat) + 1e-08)
    update = (
        jnp.dot(direction, table, precision=lax.Precision.HIGHEST) * flips_full[None, :]
        + 0.1 * master
    )
    own_weights = (master - 0.0003 * update).astype(jnp.bfloat16)
    weights = lax.all_gather(own_weights, "dp", axis=0, tiled=True)
    return (weights, update)


def solution(mesh):
    return jax.shard_map(
        local,
        mesh=mesh,
        in_specs=(
            P("dp", "mp"),
            P("dp", None),
            P(("mp", "dp"), None),
            P(("mp", "dp"), None),
            P(("mp", "dp"), None),
            P(),
            P(),
        ),
        out_specs=(P("mp", None), P(("mp", "dp"), None)),
        check_vma=False,
    )
```

profile of v0, /device:TPU:1, one launch (start us, length us, event | category | flops | bytes accessed | tf_op | source)
XLA Modules:
  0.0 335.1 jit_solution(12141799376921735877)
XLA Ops:
  7.2 0.0 copy-start
  7.2 0.0 all-gather.3.cloned.1.call-start
  7.2 0.9 fusion.33
  8.1 0.8 copy-done
  8.8 5.6 %fusion.1 = f32[1792,512]{1,0:T(8,128)} fusion(bf16[512,512]{1,0:T(8,128)(2,1)} %constant.26.clone.1, bf16[640,1792]{1,0:T(8,128)(2,1)S(1)} %copy-done, bf16[640,512]{1,0:T(8,128)(2,1)} %param.8, bf16[512]{0:T(512)(128)(2,1)S(1)} %get-tuple-element.3), kind=kOutput, calls=%fused_computation.1 | convolution fusion | flops 2117599232 | bytes 7144448 | tf_op jit(solution)/shard_map/dot_general | solution.py:29
  14.5 0.0 copy-start.1
  14.5 0.0 copy-start.2
  14.5 0.0 copy-start.4
  14.5 178.2 %fusion = f32[32,512]{1,0:T(8,128)S(1)} fusion(f32[1792,512]{1,0:T(8,128)} %fusion.1), kind=kCustom, calls=%all-reduce-scatter | all-reduce-scatter fusion | flops 1048577 | bytes 3737600
  192.7 1.3 collective-permute-start.6
  194.0 1.3 collective-permute-start.5
  195.3 1.3 collective-permute-start.7
  196.6 1.9 collective-permute-start.4
  198.5 10.8 %collective-permute-start.3 = (f32[32,512]{1,0:T(8,128)S(1)}, f32[32,512]{1,0:T(8,128)}, u32[]{:S(2)}, u32[]{:S(2)}) collective-permute-start(f32[32,512]{1,0:T(8,128)S(1)} %fusion), channel_id=1, source_target_pairs={{0,32},{8,40},{16,48},{24,56},{32,64},{40,72},{48,80},{56,88},{64,... | collective-permute-start | bytes 196616
  209.3 0.0 collective-permute-done.7
  209.3 0.0 copy-start.7
  209.3 1.9 collective-permute-start.2
  211.2 0.0 collective-permute-done.6
  211.2 0.0 copy-start.5
  211.2 8.3 %collective-permute-start.1 = (f32[32,512]{1,0:T(8,128)S(1)}, f32[32,512]{1,0:T(8,128)}, u32[]{:S(2)}, u32[]{:S(2)}) collective-permute-start(f32[32,512]{1,0:T(8,128)S(1)} %fusion), channel_id=1, source_target_pairs={{0,16},{8,24},{16,32},{24,40},{32,48},{40,56},{48,64},{56,72},{64,... | collective-permute-start | bytes 196616
  219.5 0.0 collective-permute-done.5
  219.5 0.0 copy-done.5
  219.5 0.0 copy-start.6
  219.5 2.2 collective-permute-start
  221.7 0.0 copy-done.7
  221.7 0.0 copy-done.6
  222.4 1.3 dynamic-slice.4
  224.3 0.0 collective-permute-done.4
  224.3 0.0 collective-permute-done.3
  224.4 0.0 collective-permute-done.2
  224.4 0.0 collective-permute-done.1
  224.4 0.0 collective-permute-done
  224.4 13.2 %concatenate = f32[284,512]{1,0:T(8,128)} concatenate(f32[28,512]{1,0:T(8,128)} %copy-done.7, f32[32,512]{1,0:T(8,128)} %copy-done.5, f32[32,512]{1,0:T(8,128)} %copy-done.6, f32[32,512]{1,0:T(8,128)} %collective-permute-done.4, f32[32,512]{1,0:T(8,128)} %collective-permute-done.3, f32[32,512]{1,0:T(8,128)} %collective-permute-done.2, f32[32,512]{1,0:T(8,128)} %collective-permute-done.1, ...), dimensions={0} | concatenate | bytes 1163264
  237.6 0.0 copy-done.1
  237.6 0.0 copy-done.2
  237.6 0.0 copy-done.4
  237.6 1.6 fusion.3
  239.2 0.0 copy-start.3
  239.3 0.6 fusion.17
  239.9 0.0 all-gather.3.cloned.1.call-update
  239.9 84.6 %all-gather.3.cloned.1.call-done = bf16[64,28,512]{2,1,0:T(8,128)(2,1)} async-done(((bf16[1,28,512]{2,1,0:T(8,128)(2,1)}), bf16[64,28,512]{2,1,0:T(8,128)(2,1)}) %all-gather.3.cloned.1.call-update) | async-done | bytes 1835024 | tf_op jit(solution)/shard_map/all_gather | solution.py:43
  324.5 3.7 %reshape.16 = bf16[1792,512]{1,0:T(8,128)(2,1)} reshape(bf16[64,28,512]{2,1,0:T(8,128)(2,1)} %all-gather.3.cloned.1.call-done) | data formatting | bytes 3670016
  328.3 0.0 copy-done.3
  (1 shorter events, 0.0 us)
Async XLA Ops:
  7.2 1.7 copy-start
  7.2 317.4 %all-gather.3.cloned.1.call-start = ((), (), s32[]{:S(2)}) async-start(), calls=%async_computation | async-start | bytes 2129920 | tf_op jit(solution)/shard_map/all_gather | solution.py:43
  14.5 223.1 %copy-start.1 = (f32[512,512]{1,0:T(8,128)S(1)}, f32[512,512]{1,0:T(8,128)}, u32[]{:S(2)}) copy-start(f32[512,512]{1,0:T(8,128)} %constant.35.clone.1) | copy-start | bytes 3145732
  14.5 223.1 %copy-start.2 = (f32[28,512]{1,0:T(8,128)S(1)}, f32[28,512]{1,0:T(8,128)}, u32[]{:S(2)}) copy-start(f32[28,512]{1,0:T(8,128)} %param.9) | copy-start | bytes 172036
  14.5 223.1 %copy-start.4 = (f32[28,512]{1,0:T(8,128)S(1)}, f32[28,512]{1,0:T(8,128)}, u32[]{:S(2)}) copy-start(f32[28,512]{1,0:T(8,128)} %param.11) | copy-start | bytes 172036
  192.7 18.5 %collective-permute-start.6 = (f32[32,512]{1,0:T(8,128)S(1)}, f32[32,512]{1,0:T(8,128)S(1)}, u32[]{:S(2)}, u32[]{:S(2)}) collective-permute-start(f32[32,512]{1,0:T(8,128)S(1)} %fusion), channel_id=1, source_target_pairs={{0,56},{8,64},{16,72},{24,80},{32,88},{40,96},{48,104},{56,112},{6... | collective-permute-start | bytes 196616
  194.0 25.5 %collective-permute-start.5 = (f32[32,512]{1,0:T(8,128)S(1)}, f32[32,512]{1,0:T(8,128)S(1)}, u32[]{:S(2)}, u32[]{:S(2)}) collective-permute-start(f32[32,512]{1,0:T(8,128)S(1)} %fusion), channel_id=1, source_target_pairs={{0,48},{8,56},{16,64},{24,72},{32,80},{40,88},{48,96},{56,104},{64... | collective-permute-start | bytes 196616
  195.3 14.0 %collective-permute-start.7 = (f32[28,512]{1,0:T(8,128)S(1)}, f32[28,512]{1,0:T(8,128)S(1)}, u32[]{:S(2)}, u32[]{:S(2)}) collective-permute-start(f32[28,512]{1,0:T(8,128)S(1)} %slice), channel_id=1, source_target_pairs={{0,64},{8,72},{16,80},{24,88},{32,96},{40,104},{48,112},{56,120},{... | collective-permute-start | bytes 172040
  196.6 27.8 %collective-permute-start.4 = (f32[32,512]{1,0:T(8,128)S(1)}, f32[32,512]{1,0:T(8,128)}, u32[]{:S(2)}, u32[]{:S(2)}) collective-permute-start(f32[32,512]{1,0:T(8,128)S(1)} %fusion), channel_id=1, source_target_pairs={{0,40},{8,48},{16,56},{24,64},{32,72},{40,80},{48,88},{56,96},{64,... | collective-permute-start | bytes 196616
  198.5 25.9 %collective-permute-start.3 = (f32[32,512]{1,0:T(8,128)S(1)}, f32[32,512]{1,0:T(8,128)}, u32[]{:S(2)}, u32[]{:S(2)}) collective-permute-start(f32[32,512]{1,0:T(8,128)S(1)} %fusion), channel_id=1, source_target_pairs={{0,32},{8,40},{16,48},{24,56},{32,64},{40,72},{48,80},{56,88},{64,... | collective-permute-start | bytes 196616
  209.3 12.4 %copy-start.7 = (f32[28,512]{1,0:T(8,128)}, f32[28,512]{1,0:T(8,128)S(1)}, u32[]{:S(2)}) copy-start(f32[28,512]{1,0:T(8,128)S(1)} %collective-permute-done.7) | copy-start | bytes 172036
  209.3 15.1 %collective-permute-start.2 = (f32[32,512]{1,0:T(8,128)S(1)}, f32[32,512]{1,0:T(8,128)}, u32[]{:S(2)}, u32[]{:S(2)}) collective-permute-start(f32[32,512]{1,0:T(8,128)S(1)} %fusion), channel_id=1, source_target_pairs={{0,24},{8,32},{16,40},{24,48},{32,56},{40,64},{48,72},{56,80},{64,... | collective-permute-start | bytes 196616
  211.2 8.3 %copy-start.5 = (f32[32,512]{1,0:T(8,128)}, f32[32,512]{1,0:T(8,128)S(1)}, u32[]{:S(2)}) copy-start(f32[32,512]{1,0:T(8,128)S(1)} %collective-permute-done.6) | copy-start | bytes 196612
  211.2 13.2 %collective-permute-start.1 = (f32[32,512]{1,0:T(8,128)S(1)}, f32[32,512]{1,0:T(8,128)}, u32[]{:S(2)}, u32[]{:S(2)}) collective-permute-start(f32[32,512]{1,0:T(8,128)S(1)} %fusion), channel_id=1, source_target_pairs={{0,16},{8,24},{16,32},{24,40},{32,48},{40,56},{48,64},{56,72},{64,... | collective-permute-start | bytes 196616
  219.5 2.2 copy-start.6
  219.5 4.9 %collective-permute-start = (f32[32,512]{1,0:T(8,128)S(1)}, f32[32,512]{1,0:T(8,128)}, u32[]{:S(2)}, u32[]{:S(2)}) collective-permute-start(f32[32,512]{1,0:T(8,128)S(1)} %fusion), channel_id=1, source_target_pairs={{0,8},{8,16},{16,24},{24,32},{32,40},{40,48},{48,56},{56,64},{64,7... | collective-permute-start | bytes 196616
  239.2 89.0 %copy-start.3 = (f32[28,512]{1,0:T(8,128)}, f32[28,512]{1,0:T(8,128)S(1)}, u32[]{:S(2)}) copy-start(f32[28,512]{1,0:T(8,128)S(1)} %fusion.3) | copy-start | bytes 172036
Sparse Core Ops, SparseCore 0:
  240.0 84.4 all-gather.2
where the time goes:
time: 336 us; the launch traced here: 335 us
  blocking collectives  178 us (53%)
  waiting for transfers between devices  84.7 us (25%)
  starting transfers between devices  29 us (9%)
  local copies, waits for them, and re-layouts  19 us (6%)
  between operations  15.6 us (5%)
  matrix products  7.24 us (2%)
    unnamed x1, blocking collectives  178 us
    all_gather x1, waiting for transfers between devices, local(): weights = lax.all_gather(own_weights, 'dp', axis=0, tiled=True)  84.6 us
    unnamed x8, starting transfers between devices  28.9 us
    unnamed x20, local copies, waits for them, and re-layouts  19 us
  transfers between devices with their start and end apart: 9, of which 1 were waited for; matrix products, arithmetic and copies ran while one was open for 0% of the time, Pallas kernels for 0%

commit v1 on v0

v1 whole, which is shorter than its diff:
```python
import jax
import jax.numpy as jnp
import numpy as np
from jax import lax
from jax.sharding import Mesh, PartitionSpec as P

DP = ("zh", "y", "c")
MP = ("zl", "x")


def signs_table(order):
    table = np.ones((1, 1), np.float32)
    while table.shape[0] < order:
        table = np.block([[table, table], [table, -table]])
    return table


def exact_dot(value, table):
    high = value.astype(jnp.bfloat16)
    rest = value - high.astype(jnp.float32)
    middle = rest.astype(jnp.bfloat16)
    low = (rest - middle.astype(jnp.float32)).astype(jnp.bfloat16)
    dot = lambda part: jnp.dot(part, table, preferred_element_type=jnp.float32)
    return dot(high) + (dot(middle) + dot(low))


def local(hidden, out_grad, master, moment_one, moment_two, sign_flips, step_count):
    columns = out_grad.shape[1]
    zh, y, c = (lax.axis_size(a) for a in DP)
    replicas = zh * y * c
    rows = master.shape[0]
    factor = columns ** (-0.5)
    table = jnp.asarray(signs_table(columns), jnp.bfloat16)
    flips = sign_flips.astype(jnp.float32)[None, :]
    core = lax.axis_index("c")
    partial_value = lax.dot_general(
        hidden, out_grad, (((0,), (0,)), ((), ())), preferred_element_type=jnp.float32
    ).astype(jnp.bfloat16)
    blocks = partial_value.reshape(zh, y, c, rows, columns)
    keep = lax.dynamic_index_in_dim(blocks, core, 2, keepdims=False)
    send = lax.dynamic_index_in_dim(blocks, 1 - core, 2, keepdims=False)
    got = lax.ppermute(send, "c", [(0, 1), (1, 0)])
    pair = (keep.astype(jnp.float32) + got.astype(jnp.float32)).astype(jnp.bfloat16)
    pair = jnp.swapaxes(pair, 0, 1)
    by_y = lax.all_to_all(pair, "y", 0, 0)
    by_y = jnp.sum(by_y.astype(jnp.float32), axis=0).astype(jnp.bfloat16)
    by_z = lax.all_to_all(by_y, "zh", 0, 0)
    summed = jnp.sum(by_z.astype(jnp.float32), axis=0)
    gradient = exact_dot(summed * flips, table) * (factor / replicas)
    steps_done = step_count[0].astype(jnp.float32)
    first = 0.9 * moment_one + 0.1 * gradient
    second = 0.95 * moment_two + 0.05 * gradient * gradient
    first_hat = first / (1.0 - jnp.power(jnp.float32(0.9), steps_done))
    second_hat = second / (1.0 - jnp.power(jnp.float32(0.95), steps_done))
    direction = first_hat / (jnp.sqrt(second_hat) + 1e-08)
    update = exact_dot(direction, table) * factor * flips + 0.1 * master
    own = (master - 0.0003 * update).astype(jnp.bfloat16)
    by_z = lax.all_to_all(jnp.broadcast_to(own[None], (zh, rows, columns)), "zh", 0, 0)
    by_y = lax.all_to_all(
        jnp.broadcast_to(by_z[None], (y, zh, rows, columns)), "y", 0, 0
    )
    low = lax.all_gather(by_y[: y // 2], "c", axis=0, tiled=False)
    high = lax.all_gather(by_y[y // 2 :], "c", axis=0, tiled=False)
    both = jnp.concatenate([low, high], axis=1)
    weights = jnp.transpose(both, (2, 1, 0, 3, 4)).reshape(-1, columns)
    return (weights, update)


def solution(mesh):
    inner = Mesh(mesh.devices.reshape(4, 8, 2, 2, 4), DP + MP)
    owner = P(MP + DP, None)
    return jax.shard_map(
        local,
        mesh=inner,
        in_specs=(P(DP, MP), P(DP, None), owner, owner, owner, P(), P()),
        out_specs=(P(MP, None), owner),
        check_vma=False,
    )
```

time: 336 us -> 129 us (0.38)
  blocking collectives: 178 us -> 43.9 us
  waiting for transfers between devices: 84.7 us -> 33.1 us
  between operations: 15.6 us -> 1.51 us
  starting transfers between devices: 29 us -> 22.9 us
    unnamed x1 -> x0, blocking collectives: 178 us -> none
    all_gather x1 -> x0, waiting for transfers between devices: 84.6 us -> none  [local(): weights = lax.all_gather(own_weights, 'dp', axis=0, tiled=True)]
    all_to_all x0 -> x2, blocking collectives: none -> 34.6 us  [the longest x1 24.5 us: local(): lax.all_to_all(jnp.broadcast_to(by_z[None], (y, zh, rows, columns)), 'y',...]
    all_to_all x0 -> x2, waiting for transfers between devices: none -> 30.8 us  [the longest x1 23.3 us: local(): by_y = lax.all_to_all(pair, 'y', 0, 0)]
    unnamed x8 -> x0, starting transfers between devices: 28.9 us -> none
    unnamed x20 -> x12, local copies, waits for them, and re-layouts: 19 us -> 1.68 us
    all_to_all x0 -> x2, starting transfers between devices: none -> 14.1 us  [the longest x1 9.78 us: local(): by_z = lax.all_to_all(by_y, 'zh', 0, 0)]
    all_gather x0 -> x2, blocking collectives: none -> 9.33 us  [the longest x1 6.88 us: local(): low = lax.all_gather(by_y[:y // 2], 'c', axis=0, tiled=False)]
  transfers between devices with their start and end apart: 9 -> 3, of which waited for: 1 -> 3; matrix products, arithmetic and copies ran while one was open for 0% -> 0% of each run, Pallas kernels for 0% -> 0%
where the time goes in v1:
time: 129 us; the launch traced here: 128 us
  blocking collectives  43.9 us (34%)
  waiting for transfers between devices  33.1 us (26%)
  starting transfers between devices  22.9 us (18%)
  local copies, waits for them, and re-layouts  16.7 us (13%)
  matrix products  5.8 us (4%)
  other arithmetic  4.54 us (4%)
  between operations  1.51 us (1%)
    all_to_all x1, blocking collectives, local(): lax.all_to_all(jnp.broadcast_to(by_z[None], (y, zh, rows, columns)), 'y',...  24.5 us
    all_to_all x1, waiting for transfers between devices, local(): by_y = lax.all_to_all(pair, 'y', 0, 0)  23.3 us
    all_to_all x1, blocking collectives, local(): lax.all_to_all(jnp.broadcast_to(own[None], (zh, rows, columns)), 'zh', 0, 0)  10.1 us
    all_to_all x1, starting transfers between devices, local(): by_z = lax.all_to_all(by_y, 'zh', 0, 0)  9.78 us
    ppermute x1, starting transfers between devices, local(): got = lax.ppermute(send, 'c', [(0, 1), (1, 0)])  8.77 us
    all_to_all x1, waiting for transfers between devices, local(): by_z = lax.all_to_all(by_y, 'zh', 0, 0)  7.46 us
    all_gather x1, blocking collectives, local(): low = lax.all_gather(by_y[:y // 2], 'c', axis=0, tiled=False)  6.88 us
    all_to_all x1, starting transfers between devices, local(): by_y = lax.all_to_all(pair, 'y', 0, 0)  4.35 us
  transfers between devices with their start and end apart: 3, of which 3 were waited for; matrix products, arithmetic and copies ran while one was open for 0% of the time, Pallas kernels for 0%

profile of v1, /device:TPU:1, one launch (start us, length us, event | category | flops | bytes accessed | tf_op | source)
XLA Modules:
  0.0 128.4 jit_solution(14958623056600390456)
XLA Ops:
  0.6 0.0 copy-start
  0.7 1.6 %copy-done = bf16[640,1792]{1,0:T(8,128)(2,1)S(1)} copy-done((bf16[640,1792]{1,0:T(8,128)(2,1)S(1)}, bf16[640,1792]{1,0:T(8,128)(2,1)}, u32[]{:S(2)}) %copy-start) | copy-done | bytes 2293784
  2.3 3.9 %convolution_convert_fusion = bf16[1792,512]{1,0:T(8,128)(2,1)} fusion(bf16[640,1792]{1,0:T(8,128)(2,1)S(1)} %copy-done, bf16[640,512]{1,0:T(8,128)(2,1)} %param.9), kind=kOutput, calls=%fused_computation | convolution fusion | flops 1175322624 | bytes 4784128 | tf_op jit(solution)/shard_map/dot_general | solution.py:36
  6.2 3.7 %reshape.24 = bf16[4,8,2,28,512]{4,3,2,1,0:T(8,128)(2,1)} reshape(bf16[1792,512]{1,0:T(8,128)(2,1)} %convolution_convert_fusion) | data formatting | bytes 3670016 | tf_op jit(solution)/shard_map/reshape | solution.py:39
  10.0 1.3 %constant_dynamic-slice_fusion = bf16[4,8,1,28,512]{4,3,2,1,0:T(8,128)(2,1)S(1)} fusion(bf16[4,8,2,28,512]{4,3,2,1,0:T(8,128)(2,1)} %reshape.24, s32[]{:T(128)S(6)} %select_n.8), kind=kLoop, calls=%fused_computation.29 | loop fusion | bytes 1835012 | tf_op jit(solution)/shard_map/jit(dynamic_index_in_dim)/dynamic_slice | solution.py:41
  11.3 1.4 %copy.33 = bf16[4,8,1,28,512]{4,1,3,2,0:T(8,128)(2,1)} copy(bf16[4,8,1,28,512]{4,3,2,1,0:T(8,128)(2,1)S(1)} %constant_dynamic-slice_fusion) | data formatting | bytes 1835008 | tf_op jit(solution)/shard_map/jit(dynamic_index_in_dim)/dynamic_slice | solution.py:41
  12.7 8.8 %collective-permute-start = (bf16[4,8,28,512]{3,1,2,0:T(8,128)(2,1)}, bf16[4,8,28,512]{3,1,2,0:T(8,128)(2,1)S(1)}, u32[]{:S(2)}, u32[]{:S(2)}) collective-permute-start(bf16[4,8,28,512]{3,1,2,0:T(8,128)(2,1)} %bitcast.21), channel_id=1, source_target_pairs={{0,8},{8,0},{1,9},{9,1},{2,10},{10,2},{3,11},{11,3},{4,12},{12,4},... | collective-permute-start | bytes 2752520 | tf_op jit(solution)/shard_map/ppermute | solution.py:42
  21.5 2.3 %collective-permute-done = bf16[4,8,28,512]{3,1,2,0:T(8,128)(2,1)S(1)} collective-permute-done((bf16[4,8,28,512]{3,1,2,0:T(8,128)(2,1)}, bf16[4,8,28,512]{3,1,2,0:T(8,128)(2,1)S(1)}, u32[]{:S(2)}, u32[]{:S(2)}) %collective-permute-start) | collective-permute-done | bytes 917536 | tf_op jit(solution)/shard_map/ppermute | solution.py:42
  23.8 1.7 %fusion.3 = bf16[8,4,28,512]{3,2,0,1:T(8,128)(2,1)S(1)} fusion(bf16[4,8,28,512]{3,1,2,0:T(8,128)(2,1)S(1)} %collective-permute-done, bf16[4,8,2,28,512]{4,3,2,1,0:T(8,128)(2,1)} %reshape.24, s32[]{:T(128)S(6)} %select_n.7), kind=kLoop, calls=%fused_computation.10 | loop fusion | flops 1835008 | bytes 2752516 | tf_op jit(solution)/shard_map/transpose | solution.py:44
  25.5 0.0 copy-start.3
  25.5 1.6 %copy.27 = bf16[8,4,28,512]{3,1,2,0:T(4,128)(2,1)} copy(bf16[8,4,28,512]{3,2,0,1:T(8,128)(2,1)S(1)} %fusion.3) | data formatting | bytes 1835008 | tf_op jit(solution)/shard_map/transpose | solution.py:44
  27.1 0.0 copy-start.1
  27.1 0.0 copy-start.4
  27.1 0.0 copy-start.5
  27.1 4.4 %all-to-all-start = ((bf16[8,4,28,512]{3,1,2,0:T(4,128)(2,1)}), bf16[8,4,28,512]{3,1,2,0:T(4,128)(2,1)}, u32[]{:S(2)}, u32[]{:S(2)}) async-start(bf16[8,4,28,512]{3,1,2,0:T(4,128)(2,1)} %copy.27), calls=%async_computation | async-start | bytes 1835008 | tf_op jit(solution)/shard_map/all_to_all | solution.py:45
  31.5 0.0 copy-done.3
  32.2 23.3 %all-to-all-done = bf16[8,4,28,512]{3,1,2,0:T(4,128)(2,1)} async-done(((bf16[8,4,28,512]{3,1,2,0:T(4,128)(2,1)}), bf16[8,4,28,512]{3,1,2,0:T(4,128)(2,1)}, u32[]{:S(2)}, u32[]{:S(2)}) %all-to-all-start) | async-done | bytes 917536 | tf_op jit(solution)/shard_map/all_to_all | solution.py:45
  55.6 1.6 %reduce_sum.21 = bf16[4,28,512]{2,0,1:T(4,128)(2,1)S(1)} reduce(bf16[8,4,28,512]{3,1,2,0:T(4,128)(2,1)} %all-to-all-done, bf16[]{:T(256)} %constant.40.clone.1), dimensions={0}, to_apply=%region_0.1 | reduce | flops 401408 | bytes 1032194 | tf_op jit(solution)/shard_map/reduce_sum | solution.py:46
  57.2 0.7 copy.28
  57.9 0.0 copy-start.2
  57.9 9.8 %all-to-all-start.1 = ((bf16[4,28,512]{2,1,0:T(8,128)(2,1)}), bf16[4,28,512]{2,1,0:T(8,128)(2,1)S(1)}, u32[]{:S(2)}, u32[]{:S(2)}) async-start(bf16[4,28,512]{2,1,0:T(8,128)(2,1)} %copy.28), calls=%async_computation.1 | async-start | bytes 262144 | tf_op jit(solution)/shard_map/all_to_all | solution.py:47
  67.7 7.5 %all-to-all-done.1 = bf16[4,28,512]{2,1,0:T(8,128)(2,1)S(1)} async-done(((bf16[4,28,512]{2,1,0:T(8,128)(2,1)}), bf16[4,28,512]{2,1,0:T(8,128)(2,1)S(1)}, u32[]{:S(2)}, u32[]{:S(2)}) %all-to-all-start.1) | async-done | bytes 114720 | tf_op jit(solution)/shard_map/all_to_all | solution.py:47
  75.1 0.0 copy-done.1
  75.2 0.2 fusion.9
  75.3 0.2 convolution_add_fusion.2
  75.5 0.0 copy-done.4
  75.6 0.0 copy-done.5
  75.6 0.2 multiply_divide_fusion
  75.8 0.2 fusion.7
  76.0 0.2 convolution_add_fusion
  76.2 0.0 copy-done.2
  76.2 0.8 subtract_convert_fusion
  77.1 10.1 %all_to_all.20 = bf16[4,28,512]{2,1,0:T(8,128)(2,1)S(1)} all-to-all(bf16[4,28,512]{2,1,0:T(8,128)(2,1)S(1)} %broadcast_in_dim.4), channel_id=1, replica_groups=mesh['zh'=4,'y'=8,'c'=2,'zl'=2,'x'=4] {'zh'}, dimensions={0} | all-to-all | bytes 229376 | tf_op jit(solution)/shard_map/all_to_all | solution.py:58
  87.1 0.1 copy.29
  87.2 0.2 broadcast_in_dim.5
  87.5 24.5 %all_to_all.21 = bf16[8,4,28,512]{3,1,2,0:T(4,128)(2,1)S(1)} all-to-all(bf16[8,4,28,512]{3,1,2,0:T(4,128)(2,1)S(1)} %broadcast_in_dim.5), channel_id=1, replica_groups=mesh['zh'=4,'y'=8,'c'=2,'zl'=2,'x'=4] {'y'}, dimensions={0} | all-to-all | bytes 1835008 | tf_op jit(solution)/shard_map/all_to_all | solution.py:59
  112.0 0.3 fusion.14
  112.3 6.9 %all-gather = bf16[8,4,28,512]{3,1,2,0:T(4,128)(2,1)S(1)} all-gather(bf16[4,4,28,512]{3,1,2,0:T(4,128)(2,1)S(1)} %get-tuple-element.2), channel_id=2, replica_groups=mesh['zh'=4,'y'=8,'c'=2,'zl'=2,'x'=4] {'c'}, dimensions={0}, use_global_device_ids=true | all-gather | bytes 1376256 | tf_op jit(solution)/shard_map/all_gather | solution.py:62
  119.2 2.5 %all-gather.1 = bf16[8,4,28,512]{3,1,2,0:T(4,128)(2,1)S(1)} all-gather(bf16[4,4,28,512]{3,1,2,0:T(4,128)(2,1)S(1)} %get-tuple-element.3), channel_id=3, replica_groups=mesh['zh'=4,'y'=8,'c'=2,'zl'=2,'x'=4] {'c'}, dimensions={0}, use_global_device_ids=true | all-gather | bytes 1376256 | tf_op jit(solution)/shard_map/all_gather | solution.py:63
  121.6 1.2 maximum_bitcast_fusion
  122.8 1.8 %copy.30 = bf16[4,8,2,28,512]{4,3,2,1,0:T(8,128)(2,1)} copy(bf16[4,8,2,28,512]{4,0,3,1,2:T(4,128)(2,1)S(1)} %maximum_bitcast_fusion) | data formatting | bytes 3670016 | tf_op jit(solution)/shard_map/transpose | solution.py:65
  124.6 3.7 %reshape.25 = bf16[1792,512]{1,0:T(8,128)(2,1)} reshape(bf16[4,8,2,28,512]{4,3,2,1,0:T(8,128)(2,1)} %copy.30) | data formatting | bytes 3670016 | tf_op jit(solution)/shard_map/reshape | solution.py:65
  (4 shorter events, 0.0 us)
Async XLA Ops:
  0.6 1.7 %copy-start = (bf16[640,1792]{1,0:T(8,128)(2,1)S(1)}, bf16[640,1792]{1,0:T(8,128)(2,1)}, u32[]{:S(2)}) copy-start(bf16[640,1792]{1,0:T(8,128)(2,1)} %param.8) | copy-start | bytes 6881284
  12.7 11.1 %collective-permute-start = (bf16[4,8,28,512]{3,1,2,0:T(8,128)(2,1)}, bf16[4,8,28,512]{3,1,2,0:T(8,128)(2,1)S(1)}, u32[]{:S(2)}, u32[]{:S(2)}) collective-permute-start(bf16[4,8,28,512]{3,1,2,0:T(8,128)(2,1)} %bitcast.21), channel_id=1, source_target_pairs={{0,8},{8,0},{1,9},{9,1},{2,10},{10,2},{3,11},{11,3},{4,12},{12,4},... | collective-permute-start | bytes 2752520 | tf_op jit(solution)/shard_map/ppermute | solution.py:42
  25.5 6.0 %copy-start.3 = (s32[512]{0:T(512)S(1)}, s32[512]{0:T(512)}, u32[]{:S(2)}) copy-start(s32[512]{0:T(512)} %param.13) | copy-start | bytes 6148
  27.1 48.0 %copy-start.1 = (bf16[512,512]{1,0:T(8,128)(2,1)S(1)}, bf16[512,512]{1,0:T(8,128)(2,1)}, u32[]{:S(2)}) copy-start(bf16[512,512]{1,0:T(8,128)(2,1)} %constant.53.clone) | copy-start | bytes 1572868
  27.1 48.4 %copy-start.4 = (f32[28,512]{1,0:T(8,128)S(1)}, f32[28,512]{1,0:T(8,128)}, u32[]{:S(2)}) copy-start(f32[28,512]{1,0:T(8,128)} %param.12) | copy-start | bytes 172036
  27.1 48.4 %copy-start.5 = (f32[28,512]{1,0:T(8,128)S(1)}, f32[28,512]{1,0:T(8,128)}, u32[]{:S(2)}) copy-start(f32[28,512]{1,0:T(8,128)} %param.11) | copy-start | bytes 172036
  27.1 28.4 %all-to-all-start = ((bf16[8,4,28,512]{3,1,2,0:T(4,128)(2,1)}), bf16[8,4,28,512]{3,1,2,0:T(4,128)(2,1)}, u32[]{:S(2)}, u32[]{:S(2)}) async-start(bf16[8,4,28,512]{3,1,2,0:T(4,128)(2,1)} %copy.27), calls=%async_computation | async-start | bytes 1835008 | tf_op jit(solution)/shard_map/all_to_all | solution.py:45
  57.9 18.3 %copy-start.2 = (f32[28,512]{1,0:T(8,128)S(1)}, f32[28,512]{1,0:T(8,128)}, u32[]{:S(2)}) copy-start(f32[28,512]{1,0:T(8,128)} %param.10) | copy-start | bytes 172036
  57.9 17.2 %all-to-all-start.1 = ((bf16[4,28,512]{2,1,0:T(8,128)(2,1)}), bf16[4,28,512]{2,1,0:T(8,128)(2,1)S(1)}, u32[]{:S(2)}, u32[]{:S(2)}) async-start(bf16[4,28,512]{2,1,0:T(8,128)(2,1)} %copy.28), calls=%async_computation.1 | async-start | bytes 262144 | tf_op jit(solution)/shard_map/all_to_all | solution.py:47

commit v2 on v1

v2 whole, which is shorter than its diff:
```python
import functools

import jax
import jax.numpy as jnp
import numpy as np
from jax import lax
from jax.experimental import pallas as pl
from jax.experimental.pallas import tpu as pltpu
from jax.sharding import Mesh, PartitionSpec as P

DP = ("zh", "y", "c")
MP = ("zl", "x")
LANES = 128
VMEM_LIMIT = 48 * 1024 * 1024


def signs_table(order):
    table = np.ones((1, 1), np.float32)
    while table.shape[0] < order:
        table = np.block([[table, table], [table, -table]])
    return table


def pack(block):
    parts = block.shape[1] // LANES
    return jnp.concatenate(
        [block[:, LANES * j : LANES * (j + 1)] for j in range(parts)], axis=0
    )


def unpack(block, rows):
    parts = block.shape[0] // rows
    return jnp.concatenate(
        [block[rows * j : rows * (j + 1), :] for j in range(parts)], axis=1
    )


def exact_dot(value, table):
    high = value.astype(jnp.bfloat16)
    rest = value - high.astype(jnp.float32)
    middle = rest.astype(jnp.bfloat16)
    low = (rest - middle.astype(jnp.float32)).astype(jnp.bfloat16)
    dot = lambda part: jnp.dot(part, table, preferred_element_type=jnp.float32)
    return dot(high) + (dot(middle) + dot(low))


def partial_kernel(rows, core_ref, hidden_ref, grad_ref, keep_ref, send_ref, held):
    held[...] = lax.dot_general(
        hidden_ref[...],
        grad_ref[...],
        (((0,), (0,)), ((), ())),
        preferred_element_type=jnp.float32,
    )
    first = core_ref[0] == 0
    for k in range(keep_ref.shape[0]):
        both = held[2 * rows * k : 2 * rows * (k + 1), :]
        lower, upper = pack(both[:rows]), pack(both[rows:])
        keep_ref[k] = jnp.where(first, lower, upper).astype(jnp.bfloat16)
        send_ref[k] = jnp.where(first, upper, lower).astype(jnp.bfloat16)


def partials(core, hidden, out_grad, rows, chips):
    tokens, units = hidden.shape
    columns = out_grad.shape[1]
    steps = 2
    high = rows * columns // LANES
    block = pl.BlockSpec((chips // steps, high, LANES), lambda i, core: (i, 0, 0))
    return pl.pallas_call(
        functools.partial(partial_kernel, rows),
        out_shape=[jax.ShapeDtypeStruct((chips, high, LANES), jnp.bfloat16)] * 2,
        grid_spec=pltpu.PrefetchScalarGridSpec(
            num_scalar_prefetch=1,
            grid=(steps,),
            in_specs=[
                pl.BlockSpec((tokens, units // steps), lambda i, core: (0, i)),
                pl.BlockSpec((tokens, columns), lambda i, core: (0, 0)),
            ],
            out_specs=[block, block],
            scratch_shapes=[pltpu.VMEM((units // steps, columns), jnp.float32)],
        ),
        compiler_params=pltpu.CompilerParams(vmem_limit_bytes=VMEM_LIMIT),
        name="partials",
    )(core, hidden, out_grad)


def update_kernel(
    replicas,
    step_ref,
    got_ref,
    master_ref,
    one_ref,
    two_ref,
    flips_ref,
    table_ref,
    update_ref,
    own_ref,
):
    rows, columns = master_ref.shape
    factor = columns ** (-0.5)
    table = table_ref[...]
    flips = flips_ref[...].astype(jnp.float32)
    total = got_ref[0].astype(jnp.float32)
    for k in range(1, got_ref.shape[0]):
        total = total + got_ref[k].astype(jnp.float32)
    summed = unpack(total, rows)
    gradient = exact_dot(summed * flips, table) * (factor / replicas)
    steps_done = jnp.full((1, columns), step_ref[0], jnp.int32).astype(jnp.float32)
    first = 0.9 * one_ref[...] + 0.1 * gradient
    second = 0.95 * two_ref[...] + 0.05 * gradient * gradient
    power = lambda base: jnp.power(jnp.full((1, columns), base, jnp.float32), steps_done)
    first_hat = first / (1.0 - power(0.9))
    second_hat = second / (1.0 - power(0.95))
    direction = first_hat / (jnp.sqrt(second_hat) + 1e-08)
    master = master_ref[...]
    update = exact_dot(direction, table) * factor * flips + 0.1 * master
    update_ref[...] = update
    own = pack(master - 0.0003 * update).astype(jnp.bfloat16)
    for k in range(own_ref.shape[0]):
        own_ref[k] = own


def update_step(step_count, got, master, moment_one, moment_two, flips, table, replicas):
    vmem = pl.BlockSpec(memory_space=pltpu.VMEM)
    return pl.pallas_call(
        functools.partial(update_kernel, replicas),
        out_shape=[
            jax.ShapeDtypeStruct(master.shape, jnp.float32),
            jax.ShapeDtypeStruct(got.shape, jnp.bfloat16),
        ],
        in_specs=[pl.BlockSpec(memory_space=pltpu.SMEM)] + [vmem] * 6,
        out_specs=[vmem, vmem],
        compiler_params=pltpu.CompilerParams(vmem_limit_bytes=VMEM_LIMIT),
        name="update_step",
    )(step_count, got, master, moment_one, moment_two, flips, table)


def weights_kernel(rows, core_ref, mine_ref, other_ref, out_ref):
    first = core_ref[0] == 0
    for k in range(mine_ref.shape[0]):
        mine = unpack(mine_ref[k].astype(jnp.float32), rows)
        other = unpack(other_ref[k].astype(jnp.float32), rows)
        lower = jnp.where(first, mine, other)
        upper = jnp.where(first, other, mine)
        both = jnp.concatenate([lower, upper], axis=0).astype(jnp.bfloat16)
        out_ref[2 * rows * k : 2 * rows * (k + 1), :] = both


def weights_step(core, mine, other, rows, columns):
    chips, high, _ = mine.shape
    steps = 4
    block = pl.BlockSpec((chips // steps, high, LANES), lambda i, core: (i, 0, 0))
    return pl.pallas_call(
        functools.partial(weights_kernel, rows),
        out_shape=jax.ShapeDtypeStruct((2 * rows * chips, columns), jnp.bfloat16),
        grid_spec=pltpu.PrefetchScalarGridSpec(
            num_scalar_prefetch=1,
            grid=(steps,),
            in_specs=[block, block],
            out_specs=pl.BlockSpec(
                (2 * rows * chips // steps, columns), lambda i, core: (i, 0)
            ),
        ),
        compiler_params=pltpu.CompilerParams(vmem_limit_bytes=VMEM_LIMIT),
        name="weights_step",
    )(core, mine, other)


def local(hidden, out_grad, master, moment_one, moment_two, sign_flips, step_count):
    columns = out_grad.shape[1]
    zh, y, c = (lax.axis_size(a) for a in DP)
    rows = master.shape[0]
    swap = [(0, 1), (1, 0)]
    core = lax.axis_index("c").astype(jnp.int32)[None]
    table = jnp.asarray(signs_table(columns), jnp.bfloat16)
    keep, send = partials(core, hidden, out_grad, rows, zh * y)
    met = lax.ppermute(send, "c", swap)
    pair = (keep.astype(jnp.float32) + met.astype(jnp.float32)).astype(jnp.bfloat16)
    got = lax.all_to_all(pair, ("zh", "y"), 0, 0)
    update, own = update_step(
        step_count,
        got,
        master,
        moment_one,
        moment_two,
        sign_flips[None, :],
        table,
        zh * y * c,
    )
    mine = lax.all_to_all(own, ("zh", "y"), 0, 0)
    other = lax.ppermute(mine, "c", swap)
    return (weights_step(core, mine, other, rows, columns), update)


def solution(mesh):
    inner = Mesh(mesh.devices.reshape(4, 8, 2, 2, 4), DP + MP)
    owner = P(MP + DP, None)
    return jax.shard_map(
        local,
        mesh=inner,
        in_specs=(P(DP, MP), P(DP, None), owner, owner, owner, P(), P()),
        out_specs=(P(MP, None), owner),
        check_vma=False,
    )
```

time: 129 us -> 98.9 us (0.77)
  local copies, waits for them, and re-layouts: 16.7 us -> 2.75 us
  blocking collectives: 43.9 us -> 34.1 us
  matrix products: 5.8 us -> 0 us
  Pallas kernels: 0 us -> 5.54 us
  waiting for transfers between devices: 33.1 us -> 27.8 us
  other arithmetic: 4.54 us -> 1.16 us
  starting transfers between devices: 22.9 us -> 25 us
    all_gather x2 -> x0, blocking collectives: 9.33 us -> none  [the longest x1 6.88 us: local(): low = lax.all_gather(by_y[:y // 2], 'c', axis=0, tiled=False)]
    reshape x2 -> x0, local copies, waits for them, and re-layouts: 7.47 us -> none  [the longest x1 3.74 us: local(): weights = jnp.transpose(both, (2, 1, 0, 3, 4)).reshape(-1, columns)]
    all_to_all x2 -> x1, waiting for transfers between devices: 30.8 us -> 23.7 us  [local(): got = lax.all_to_all(pair, ('zh', 'y'), 0, 0)]
    ppermute x1 -> x2, starting transfers between devices: 8.77 us -> 14.7 us  [the longest x1 8.79 us: local(): met = lax.ppermute(send, 'c', swap)]
    dot_general x7 -> x0, matrix products: 5.8 us -> none  [the longest x1 3.94 us: local(): lax.dot_general(hidden, out_grad, (((0,), (0,)), ((), ())), preferred_ele...]
    pallas_call x0 -> x3, Pallas kernels: none -> 5.54 us  [the longest x1 2.07 us: partials(): pl.pallas_call(functools.partial(partial_kernel, rows), out_shape=[jax.Sh...]
    all_to_all x2 -> x1, starting transfers between devices: 14.1 us -> 10.3 us  [local(): got = lax.all_to_all(pair, ('zh', 'y'), 0, 0)]
    transpose x2 -> x0, local copies, waits for them, and re-layouts: 3.46 us -> none  [the longest x1 1.82 us: local(): weights = jnp.transpose(both, (2, 1, 0, 3, 4)).reshape(-1, columns)]
where the time goes in v2:
time: 98.9 us; the launch traced here: 97.7 us
  blocking collectives  34.1 us (34%)
  waiting for transfers between devices  27.8 us (28%)
  starting transfers between devices  25 us (25%)
  Pallas kernels  5.54 us (6%)
  local copies, waits for them, and re-layouts  2.75 us (3%)
  between operations  1.35 us (1%)
  other arithmetic  1.16 us (1%)
    all_to_all x1, blocking collectives, local(): mine = lax.all_to_all(own, ('zh', 'y'), 0, 0)  34.1 us
    all_to_all x1, waiting for transfers between devices, local(): got = lax.all_to_all(pair, ('zh', 'y'), 0, 0)  23.7 us
    all_to_all x1, starting transfers between devices, local(): got = lax.all_to_all(pair, ('zh', 'y'), 0, 0)  10.3 us
    ppermute x1, starting transfers between devices, local(): met = lax.ppermute(send, 'c', swap)  8.79 us
    ppermute x1, starting transfers between devices, local(): other = lax.ppermute(mine, 'c', swap)  5.91 us
    unnamed x14, local copies, waits for them, and re-layouts  2.75 us
    ppermute x1, waiting for transfers between devices, local(): met = lax.ppermute(send, 'c', swap)  2.08 us
    ppermute x1, waiting for transfers between devices, local(): other = lax.ppermute(mine, 'c', swap)  2.08 us
  transfers between devices with their start and end apart: 3, of which 3 were waited for; matrix products, arithmetic and copies ran while one was open for 0% of the time, Pallas kernels for 0%

profile of v2, /device:TPU:1, one launch (start us, length us, event | category | flops | bytes accessed | tf_op | source)
XLA Modules:
  0.0 97.7 jit_solution(681052788131347450)
XLA Ops:
  0.6 0.0 copy-start
  0.6 1.6 %copy-done = bf16[640,1792]{1,0:T(8,128)(2,1)S(1)} copy-done((bf16[640,1792]{1,0:T(8,128)(2,1)S(1)}, bf16[640,1792]{1,0:T(8,128)(2,1)}, u32[]{:S(2)}) %copy-start) | copy-done | bytes 2293784
  2.3 0.0 copy-start.1
  2.3 1.1 %copy-done.1 = bf16[640,512]{1,0:T(8,128)(2,1)S(1)} copy-done((bf16[640,512]{1,0:T(8,128)(2,1)S(1)}, bf16[640,512]{1,0:T(8,128)(2,1)}, u32[]{:S(2)}) %copy-start.1) | copy-done | bytes 655384
  3.4 2.1 %partials.1 = (bf16[32,112,128]{2,1,0:T(8,128)(2,1)S(1)}, bf16[32,112,128]{2,1,0:T(8,128)(2,1)S(1)}) custom-call(s32[1]{0:T(128)} %bitcast.core_ref, bf16[640,1792]{1,0:T(8,128)(2,1)S(1)} %copy-done, bf16[640,512]{1,0:T(8,128)(2,1)S(1)} %copy-done.1), custom_call_target="tpu_custom_call" | custom-call | tf_op jit(solution)/shard_map/partials/pallas_call | solution.py:68
  5.4 8.8 %collective-permute-start = (bf16[32,112,128]{2,1,0:T(8,128)(2,1)S(1)}, bf16[32,112,128]{2,1,0:T(8,128)(2,1)S(1)}, u32[]{:S(2)}, u32[]{:S(2)}) collective-permute-start(bf16[32,112,128]{2,1,0:T(8,128)(2,1)S(1)} %get-tuple-element.7), channel_id=1, source_target_pairs={{0,8},{8,0},{1,9},{9,1},{2,10},{10,2},{3,11},{11,3},{4,12},{12,4},... | collective-permute-start | bytes 2752520 | tf_op jit(solution)/shard_map/ppermute | solution.py:176
  14.2 2.1 %collective-permute-done = bf16[32,112,128]{2,1,0:T(8,128)(2,1)S(1)} collective-permute-done((bf16[32,112,128]{2,1,0:T(8,128)(2,1)S(1)}, bf16[32,112,128]{2,1,0:T(8,128)(2,1)S(1)}, u32[]{:S(2)}, u32[]{:S(2)}) %collective-permute-start) | collective-permute-done | bytes 917536 | tf_op jit(solution)/shard_map/ppermute | solution.py:176
  16.3 0.0 copy-start.2
  16.3 0.0 copy-start.3
  16.3 0.0 copy-start.4
  16.3 0.0 copy-start.5
  16.3 0.0 copy-start.6
  16.3 1.2 %add_convert_fusion = bf16[32,112,128]{2,1,0:T(8,128)(2,1)} fusion(bf16[32,112,128]{2,1,0:T(8,128)(2,1)S(1)} %collective-permute-done, bf16[32,112,128]{2,1,0:T(8,128)(2,1)S(1)} %get-tuple-element.6), kind=kLoop, calls=%fused_computation | loop fusion | flops 1835008 | bytes 2752512 | tf_op jit(solution)/shard_map/convert_element_type | solution.py:177
  17.5 10.3 %all-to-all-start = ((bf16[32,112,128]{2,1,0:T(8,128)(2,1)}), bf16[32,112,128]{2,1,0:T(8,128)(2,1)S(1)}, u32[]{:S(2)}, u32[]{:S(2)}) async-start(bf16[32,112,128]{2,1,0:T(8,128)(2,1)} %add_convert_fusion), calls=%async_computation | async-start | bytes 1835008 | tf_op jit(solution)/shard_map/all_to_all | solution.py:178
  28.5 23.7 %all-to-all-done.got_ref = bf16[32,112,128]{2,1,0:T(8,128)(2,1)S(1)} async-done(((bf16[32,112,128]{2,1,0:T(8,128)(2,1)}), bf16[32,112,128]{2,1,0:T(8,128)(2,1)S(1)}, u32[]{:S(2)}, u32[]{:S(2)}) %all-to-all-start) | async-done | bytes 917536 | tf_op jit(solution)/shard_map/all_to_all | solution.py:178
  52.2 0.0 copy-done.2
  52.2 0.0 copy-done.3
  52.2 0.0 copy-done.4
  52.2 0.0 copy-done.5
  52.2 0.0 copy-done.6
  52.2 1.5 %update_step.1 = (f32[28,512]{1,0:T(8,128)}, bf16[32,112,128]{2,1,0:T(8,128)(2,1)S(1)}) custom-call(s32[1]{0:T(128)S(6)} %copy.10.step_ref, bf16[32,112,128]{2,1,0:T(8,128)(2,1)S(1)} %all-to-all-done.got_ref, f32[28,512]{1,0:T(8,128)S(1)} %copy-done.3, f32[28,512]{1,0:T(8,128)S(1)} %copy-done.4, f32[28,512]{1,0:T(8,128)S(1)} %copy-done.5, ...), custom_call_target="tpu_custom_call" | custom-call | tf_op jit(solution)/shard_map/update_step/pallas_call | solution.py:124
  53.7 34.1 %all_to_all.10.mine_ref = bf16[32,112,128]{2,1,0:T(8,128)(2,1)S(1)} all-to-all(bf16[32,112,128]{2,1,0:T(8,128)(2,1)S(1)} %get-tuple-element.8), channel_id=1, replica_groups=mesh['zh'=4,'y'=8,'c'=2,'zl'=2,'x'=4] {'zh','y'}, dimensions={0} | all-to-all | bytes 1835008 | tf_op jit(solution)/shard_map/all_to_all | solution.py:189
  87.7 5.9 %collective-permute-start.1 = (bf16[32,112,128]{2,1,0:T(8,128)(2,1)S(1)}, bf16[32,112,128]{2,1,0:T(8,128)(2,1)S(1)}, u32[]{:S(2)}, u32[]{:S(2)}) collective-permute-start(bf16[32,112,128]{2,1,0:T(8,128)(2,1)S(1)} %all_to_all.10.mine_ref), channel_id=1, source_target_pairs={{0,8},{8,0},{1,9},{9,1},{2,10},{10,2},{3,11},{11,3},{4,12},{12,4},... | collective-permute-start | bytes 2752520 | tf_op jit(solution)/shard_map/ppermute | solution.py:190
  93.7 2.1 %collective-permute-done.1.other_ref = bf16[32,112,128]{2,1,0:T(8,128)(2,1)S(1)} collective-permute-done((bf16[32,112,128]{2,1,0:T(8,128)(2,1)S(1)}, bf16[32,112,128]{2,1,0:T(8,128)(2,1)S(1)}, u32[]{:S(2)}, u32[]{:S(2)}) %collective-permute-start.1) | collective-permute-done | bytes 917536 | tf_op jit(solution)/shard_map/ppermute | solution.py:190
  95.7 2.0 %weights_step.1 = bf16[1792,512]{1,0:T(8,128)(2,1)} custom-call(s32[1]{0:T(128)} %bitcast.core_ref, bf16[32,112,128]{2,1,0:T(8,128)(2,1)S(1)} %all_to_all.10.mine_ref, bf16[32,112,128]{2,1,0:T(8,128)(2,1)S(1)} %collective-permute-done.1.other_ref), custom_call_target="tpu_custom_call" | custom-call | tf_op jit(solution)/shard_map/weights_step/pallas_call | solution.py:152
Async XLA Ops:
  0.6 1.6 %copy-start = (bf16[640,1792]{1,0:T(8,128)(2,1)S(1)}, bf16[640,1792]{1,0:T(8,128)(2,1)}, u32[]{:S(2)}) copy-start(bf16[640,1792]{1,0:T(8,128)(2,1)} %hidden_ref.1) | copy-start | bytes 6881284
  2.3 1.1 %copy-start.1 = (bf16[640,512]{1,0:T(8,128)(2,1)S(1)}, bf16[640,512]{1,0:T(8,128)(2,1)}, u32[]{:S(2)}) copy-start(bf16[640,512]{1,0:T(8,128)(2,1)} %grad_ref.1) | copy-start | bytes 1966084
  5.4 10.9 %collective-permute-start = (bf16[32,112,128]{2,1,0:T(8,128)(2,1)S(1)}, bf16[32,112,128]{2,1,0:T(8,128)(2,1)S(1)}, u32[]{:S(2)}, u32[]{:S(2)}) collective-permute-start(bf16[32,112,128]{2,1,0:T(8,128)(2,1)S(1)} %get-tuple-element.7), channel_id=1, source_target_pairs={{0,8},{8,0},{1,9},{9,1},{2,10},{10,2},{3,11},{11,3},{4,12},{12,4},... | collective-permute-start | bytes 2752520 | tf_op jit(solution)/shard_map/ppermute | solution.py:176
  16.3 35.8 %copy-start.2 = (bf16[512,512]{1,0:T(8,128)(2,1)S(1)}, bf16[512,512]{1,0:T(8,128)(2,1)}, u32[]{:S(2)}) copy-start(bf16[512,512]{1,0:T(8,128)(2,1)} %constant.8.clone.table_ref) | copy-start | bytes 1572868
  16.3 35.8 %copy-start.3 = (f32[28,512]{1,0:T(8,128)S(1)}, f32[28,512]{1,0:T(8,128)}, u32[]{:S(2)}) copy-start(f32[28,512]{1,0:T(8,128)} %master_ref.1) | copy-start | bytes 172036
  16.3 35.8 %copy-start.4 = (f32[28,512]{1,0:T(8,128)S(1)}, f32[28,512]{1,0:T(8,128)}, u32[]{:S(2)}) copy-start(f32[28,512]{1,0:T(8,128)} %one_ref.1) | copy-start | bytes 172036
  16.3 35.8 %copy-start.5 = (f32[28,512]{1,0:T(8,128)S(1)}, f32[28,512]{1,0:T(8,128)}, u32[]{:S(2)}) copy-start(f32[28,512]{1,0:T(8,128)} %two_ref.1) | copy-start | bytes 172036
  16.3 35.8 %copy-start.6 = (s32[512]{0:T(512)S(1)}, s32[512]{0:T(512)}, u32[]{:S(2)}) copy-start(s32[512]{0:T(512)} %param.13) | copy-start | bytes 6148
  17.5 34.6 %all-to-all-start = ((bf16[32,112,128]{2,1,0:T(8,128)(2,1)}), bf16[32,112,128]{2,1,0:T(8,128)(2,1)S(1)}, u32[]{:S(2)}, u32[]{:S(2)}) async-start(bf16[32,112,128]{2,1,0:T(8,128)(2,1)} %add_convert_fusion), calls=%async_computation | async-start | bytes 1835008 | tf_op jit(solution)/shard_map/all_to_all | solution.py:178
  87.7 8.0 %collective-permute-start.1 = (bf16[32,112,128]{2,1,0:T(8,128)(2,1)S(1)}, bf16[32,112,128]{2,1,0:T(8,128)(2,1)S(1)}, u32[]{:S(2)}, u32[]{:S(2)}) collective-permute-start(bf16[32,112,128]{2,1,0:T(8,128)(2,1)S(1)} %all_to_all.10.mine_ref), channel_id=1, source_target_pairs={{0,8},{8,0},{1,9},{9,1},{2,10},{10,2},{3,11},{11,3},{4,12},{12,4},... | collective-permute-start | bytes 2752520 | tf_op jit(solution)/shard_map/ppermute | solution.py:190

commit v3 on v2

v3 whole, which is shorter than its diff:
```python
import functools

import jax
import jax.numpy as jnp
import numpy as np
from jax import lax
from jax.experimental import pallas as pl
from jax.experimental.pallas import tpu as pltpu
from jax.sharding import Mesh, PartitionSpec as P

DP = ("zh", "y", "c")
MP = ("zl", "x")
LANES = 128
VMEM_LIMIT = 48 * 1024 * 1024
PARTIAL_VMEM = 103 * 512 * 1024
WIDEN = 2.0**17


def signs_table(order):
    table = np.ones((1, 1), np.float32)
    while table.shape[0] < order:
        table = np.block([[table, table], [table, -table]])
    return table


def pack(block):
    parts = block.shape[1] // LANES
    return jnp.concatenate(
        [block[:, LANES * j : LANES * (j + 1)] for j in range(parts)], axis=0
    )


def unpack(block, rows):
    parts = block.shape[0] // rows
    return jnp.concatenate(
        [block[rows * j : rows * (j + 1), :] for j in range(parts)], axis=1
    )


def exact_dot(value, table):
    rows = value.shape[0]
    high = value.astype(jnp.bfloat16)
    rest = value - high.astype(jnp.float32)
    middle = rest.astype(jnp.bfloat16)
    low = (rest - middle.astype(jnp.float32)).astype(jnp.bfloat16)
    parts = jnp.dot(
        jnp.concatenate([high, middle, low], axis=0),
        table,
        preferred_element_type=jnp.float32,
    )
    return parts[:rows] + (parts[rows : 2 * rows] + parts[2 * rows :])


def partial_kernel(
    rows,
    cuts,
    step_ref,
    hidden_ref,
    grad_ref,
    keep_ref,
    send_ref,
    powers_ref,
    units,
    grad,
    held,
    sems,
):
    moves = [pltpu.make_async_copy(grad_ref, grad, sems.at[len(cuts)])]
    for i, (start, stop) in enumerate(cuts):
        moves.append(
            pltpu.make_async_copy(
                hidden_ref.at[:, start:stop], units.at[:, start:stop], sems.at[i]
            )
        )
    for move in moves:
        move.start()
    moves[0].wait()
    first = lax.axis_index("c") == 0
    done = 0
    for (start, stop), move in zip(cuts, moves[1:]):
        move.wait()
        held[start:stop, :] = lax.dot_general(
            units[:, start:stop],
            grad[...],
            (((0,), (0,)), ((), ())),
            preferred_element_type=jnp.float32,
        )
        while 2 * rows * (done + 1) <= stop:
            both = held[2 * rows * done : 2 * rows * (done + 1), :]
            lower, upper = pack(both[:rows]), pack(both[rows:])
            keep_ref[done] = jnp.where(first, lower, upper).astype(jnp.bfloat16)
            send_ref[done] = jnp.where(first, upper, lower).astype(jnp.bfloat16)
            done += 1
    shape = powers_ref.shape[1:]
    steps_done = jnp.broadcast_to(step_ref[...], shape).astype(jnp.float32)
    for i, base in enumerate((0.9, 0.95)):
        powers_ref[i] = jnp.power(jnp.full(shape, base, jnp.float32), steps_done)


def partials(step_count, hidden, out_grad, rows, chips):
    tokens, units = hidden.shape
    columns = out_grad.shape[1]
    high = rows * columns // LANES
    step = 896
    cuts = [(at, min(at + step, units)) for at in range(0, units, step)]
    vmem = pl.BlockSpec(memory_space=pltpu.VMEM)
    hbm = pl.BlockSpec(memory_space=pltpu.HBM)
    block = jax.ShapeDtypeStruct((chips, high, LANES), jnp.bfloat16)
    return pl.pallas_call(
        functools.partial(partial_kernel, rows, cuts),
        out_shape=[block, block, jax.ShapeDtypeStruct((2, 8, LANES), jnp.float32)],
        in_specs=[vmem, hbm, hbm],
        out_specs=[vmem, vmem, vmem],
        scratch_shapes=[
            pltpu.VMEM((tokens, units), jnp.bfloat16),
            pltpu.VMEM((tokens, columns), jnp.bfloat16),
            pltpu.VMEM((units, columns), jnp.float32),
            pltpu.SemaphoreType.DMA((len(cuts) + 1,)),
        ],
        compiler_params=pltpu.CompilerParams(vmem_limit_bytes=PARTIAL_VMEM),
        name="partials",
    )(step_count, hidden, out_grad)


def update_kernel(
    replicas,
    powers_ref,
    got_ref,
    master_ref,
    one_ref,
    two_ref,
    flips_ref,
    table_ref,
    update_ref,
    own_ref,
):
    rows, columns = master_ref.shape
    factor = columns ** (-0.5)
    table = table_ref[...]
    flips = flips_ref[...].astype(jnp.float32)
    total = got_ref[0].astype(jnp.float32)
    for k in range(1, got_ref.shape[0]):
        total = total + got_ref[k].astype(jnp.float32)
    summed = unpack(total, rows)
    gradient = exact_dot(summed * flips, table) * (factor / replicas)
    first = 0.9 * one_ref[...] + 0.1 * gradient
    second = 0.95 * two_ref[...] + 0.05 * gradient * gradient
    spread = lambda i: jnp.concatenate(
        [powers_ref[i, :1, :]] * (columns // LANES), axis=1
    )
    first_hat = first / (1.0 - spread(0))
    second_hat = second / (1.0 - spread(1))
    direction = first_hat / (jnp.sqrt(second_hat) + 1e-08)
    master = master_ref[...]
    update = exact_dot(direction, table) * factor * flips + 0.1 * master
    update_ref[...] = update
    own_ref[...] = (master - 0.0003 * update).astype(jnp.bfloat16).astype(jnp.float32)


def update_step(powers, got, master, moment_one, moment_two, flips, table, replicas):
    vmem = pl.BlockSpec(memory_space=pltpu.VMEM)
    return pl.pallas_call(
        functools.partial(update_kernel, replicas),
        out_shape=[jax.ShapeDtypeStruct(master.shape, jnp.float32)] * 2,
        in_specs=[vmem] * 7,
        out_specs=[vmem, vmem],
        compiler_params=pltpu.CompilerParams(vmem_limit_bytes=VMEM_LIMIT),
        name="update_step",
    )(powers, got, master, moment_one, moment_two, flips, table)


def local(hidden, out_grad, master, moment_one, moment_two, sign_flips, step_count):
    columns = out_grad.shape[1]
    zh, y, c = (lax.axis_size(a) for a in DP)
    rows = master.shape[0]
    swap = [(0, 1), (1, 0)]
    table = jnp.asarray(signs_table(columns), jnp.bfloat16)
    keep, send, powers = partials(step_count[None, :], hidden, out_grad, rows, zh * y)
    met = lax.ppermute(send, "c", swap)
    pair = (keep.astype(jnp.float32) + met.astype(jnp.float32)).astype(jnp.bfloat16)
    got = lax.all_to_all(pair, ("zh", "y"), 0, 0)
    update, own = update_step(
        powers,
        got,
        master,
        moment_one,
        moment_two,
        sign_flips[None, :],
        table,
        zh * y * c,
    )
    own = (own * WIDEN).astype(jnp.float16)
    by_z = lax.all_to_all(jnp.broadcast_to(own[None], (zh, rows, columns)), "zh", 0, 0)
    whole = lax.all_gather(by_z, ("y", "c"), axis=1, tiled=True)
    weights = (whole.astype(jnp.float32) * (1.0 / WIDEN)).astype(jnp.bfloat16)
    return (weights.reshape(-1, columns), update)


def solution(mesh):
    inner = Mesh(mesh.devices.reshape(4, 8, 2, 2, 4), DP + MP)
    owner = P(MP + DP, None)
    return jax.shard_map(
        local,
        mesh=inner,
        in_specs=(P(DP, MP), P(DP, None), owner, owner, owner, P(), P()),
        out_specs=(P(MP, None), owner),
        check_vma=False,
    )
```

time: 98.9 us -> 92.2 us (0.932)
  blocking collectives: 34.1 us -> 71.9 us
  waiting for transfers between devices: 27.8 us -> 2.08 us
  starting transfers between devices: 25 us -> 8.79 us
  local copies, waits for them, and re-layouts: 2.75 us -> 1.21 us
  Pallas kernels: 5.54 us -> 4.54 us
    all_gather x0 -> x1, blocking collectives: none -> 26.9 us  [local(): whole = lax.all_gather(by_z, ('y', 'c'), axis=1, tiled=True)]
    all_to_all x1 -> x0, waiting for transfers between devices: 23.7 us -> none  [local(): got = lax.all_to_all(pair, ('zh', 'y'), 0, 0)]
    all_to_all x1 -> x2, blocking collectives: 34.1 us -> 45 us  [the longest x1 34.4 us: local(): got = lax.all_to_all(pair, ('zh', 'y'), 0, 0)]
    all_to_all x1 -> x0, starting transfers between devices: 10.3 us -> none  [local(): got = lax.all_to_all(pair, ('zh', 'y'), 0, 0)]
    ppermute x1 -> x0, starting transfers between devices: 5.91 us -> none  [local(): other = lax.ppermute(mine, 'c', swap)]
    ppermute x1 -> x0, waiting for transfers between devices: 2.08 us -> none  [local(): other = lax.ppermute(mine, 'c', swap)]
    convert_element_type x0 -> x2, other arithmetic: none -> 1.79 us  [the longest x1 1.78 us: local(): weights = (whole.astype(jnp.float32) * (1.0 / WIDEN)).astype(jnp.bfloat16)]
    unnamed x14 -> x12, local copies, waits for them, and re-layouts: 2.75 us -> 1.1 us
  transfers between devices with their start and end apart: 3 -> 1, of which waited for: 3 -> 1; matrix products, arithmetic and copies ran while one was open for 0% -> 0% of each run, Pallas kernels for 0% -> 0%
where the time goes in v3:
time: 92.2 us; the launch traced here: 92 us
  blocking collectives  71.9 us (78%)
  starting transfers between devices  8.79 us (10%)
  Pallas kernels  4.54 us (5%)
  waiting for transfers between devices  2.08 us (2%)
  other arithmetic  2.08 us (2%)
  between operations  1.35 us (1%)
  local copies, waits for them, and re-layouts  1.21 us (1%)
    all_to_all x1, blocking collectives, local(): got = lax.all_to_all(pair, ('zh', 'y'), 0, 0)  34.4 us
    all_gather x1, blocking collectives, local(): whole = lax.all_gather(by_z, ('y', 'c'), axis=1, tiled=True)  26.9 us
    all_to_all x1, blocking collectives, local(): lax.all_to_all(jnp.broadcast_to(own[None], (zh, rows, columns)), 'zh', 0, 0)  10.6 us
    ppermute x1, starting transfers between devices, local(): met = lax.ppermute(send, 'c', swap)  8.79 us
    pallas_call x1, Pallas kernels, partials(): pl.pallas_call(functools.partial(partial_kernel, rows, cuts), out_shape=[...  3.31 us
    ppermute x1, waiting for transfers between devices, local(): met = lax.ppermute(send, 'c', swap)  2.08 us
  transfers between devices with their start and end apart: 1, of which 1 were waited for; matrix products, arithmetic and copies ran while one was open for 0% of the time, Pallas kernels for 0%

profile of v3, /device:TPU:1, one launch (start us, length us, event | category | flops | bytes accessed | tf_op | source)
XLA Modules:
  0.0 92.0 jit_solution(8954219636793811544)
XLA Ops:
  1.3 0.0 copy-start
  1.3 1.1 %copy-done = bf16[640,512]{1,0:T(8,128)(2,1)S(1)} copy-done((bf16[640,512]{1,0:T(8,128)(2,1)S(1)}, bf16[640,512]{1,0:T(8,128)(2,1)}, u32[]{:S(2)}) %copy-start) | copy-done | bytes 655384
  2.4 3.3 %partials.1 = (bf16[32,112,128]{2,1,0:T(8,128)(2,1)S(1)}, bf16[32,112,128]{2,1,0:T(8,128)(2,1)S(1)}, f32[2,8,128]{2,1,0:T(8,128)S(1)}) custom-call(s32[1,1]{1,0:T(1,128)} %bitcast.3.step_ref, bf16[640,1792]{1,0:T(8,128)(2,1)} %hidden_ref.1, bf16[640,512]{1,0:T(8,128)(2,1)S(1)} %copy-done), custom_call_target="tpu_custom_call" | custom-call | tf_op jit(solution)/shard_map/partials/pallas_call | solution.py:109
  5.7 8.8 %collective-permute-start = (bf16[32,112,128]{2,1,0:T(8,128)(2,1)S(1)}, bf16[32,112,128]{2,1,0:T(8,128)(2,1)S(1)}, u32[]{:S(2)}, u32[]{:S(2)}) collective-permute-start(bf16[32,112,128]{2,1,0:T(8,128)(2,1)S(1)} %get-tuple-element.9), channel_id=1, source_target_pairs={{0,8},{8,0},{1,9},{9,1},{2,10},{10,2},{3,11},{11,3},{4,12},{12,4},... | collective-permute-start | bytes 2752520 | tf_op jit(solution)/shard_map/ppermute | solution.py:179
  14.5 2.1 %collective-permute-done = bf16[32,112,128]{2,1,0:T(8,128)(2,1)S(1)} collective-permute-done((bf16[32,112,128]{2,1,0:T(8,128)(2,1)S(1)}, bf16[32,112,128]{2,1,0:T(8,128)(2,1)S(1)}, u32[]{:S(2)}, u32[]{:S(2)}) %collective-permute-start) | collective-permute-done | bytes 917536 | tf_op jit(solution)/shard_map/ppermute | solution.py:179
  16.6 0.0 copy-start.1
  16.6 0.0 copy-start.2
  16.6 0.0 copy-start.3
  16.6 0.0 copy-start.4
  16.6 0.0 copy-start.5
  16.6 0.3 add_convert_fusion
  16.9 34.4 %all_to_all.10.got_ref = bf16[32,112,128]{2,1,0:T(8,128)(2,1)S(1)} all-to-all(bf16[32,112,128]{2,1,0:T(8,128)(2,1)S(1)} %add_convert_fusion), channel_id=1, replica_groups=mesh['zh'=4,'y'=8,'c'=2,'zl'=2,'x'=4] {'zh','y'}, dimensions={0} | all-to-all | bytes 1835008 | tf_op jit(solution)/shard_map/all_to_all | solution.py:181
  51.3 0.0 copy-done.1
  51.3 0.0 copy-done.2
  51.3 0.0 copy-done.3
  51.3 0.0 copy-done.4
  51.3 0.0 copy-done.5
  51.3 1.2 %update_step.1 = (f32[28,512]{1,0:T(8,128)}, f32[28,512]{1,0:T(8,128)S(1)}) custom-call(f32[2,8,128]{2,1,0:T(8,128)S(1)} %get-tuple-element.7.powers_ref, bf16[32,112,128]{2,1,0:T(8,128)(2,1)S(1)} %all_to_all.10.got_ref, f32[28,512]{1,0:T(8,128)S(1)} %copy-done.2, f32[28,512]{1,0:T(8,128)S(1)} %copy-done.3, f32[28,512]{1,0:T(8,128)S(1)} %copy-done.4, ...), custom_call_target="tpu_custom_call" | custom-call | tf_op jit(solution)/shard_map/update_step/pallas_call | solution.py:162
  52.6 10.6 %all_to_all.11 = f16[4,28,512]{2,1,0:T(8,128)(2,1)S(1)} all-to-all(f16[4,28,512]{2,1,0:T(8,128)(2,1)S(1)} %broadcast_in_dim.14), channel_id=1, replica_groups=mesh['zh'=4,'y'=8,'c'=2,'zl'=2,'x'=4] {'zh'}, dimensions={0} | all-to-all | bytes 229376 | tf_op jit(solution)/shard_map/all_to_all | solution.py:193
  63.2 0.1 copy.11
  63.3 26.9 %all-gather.1 = f16[4,448,512]{2,0,1:T(4,128)(2,1)S(1)} all-gather(f16[4,28,512]{2,0,1:T(4,128)(2,1)S(1)} %copy.11), channel_id=1, replica_groups=mesh['zh'=4,'y'=8,'c'=2,'zl'=2,'x'=4] {'y','c'}, dimensions={1}, use_global_device_ids=true | all-gather | bytes 1949696 | tf_op jit(solution)/shard_map/all_gather | solution.py:194
  90.2 1.8 %multiply_convert_fusion = bf16[4,448,512]{2,1,0:T(8,128)(2,1)} fusion(f16[4,448,512]{2,0,1:T(4,128)(2,1)S(1)} %all-gather.1), kind=kLoop, calls=%fused_computation | loop fusion | flops 2752512 | bytes 3670016 | tf_op jit(solution)/shard_map/convert_element_type | solution.py:195
  (2 shorter events, 0.0 us)
Async XLA Ops:
  1.3 1.1 %copy-start = (bf16[640,512]{1,0:T(8,128)(2,1)S(1)}, bf16[640,512]{1,0:T(8,128)(2,1)}, u32[]{:S(2)}) copy-start(bf16[640,512]{1,0:T(8,128)(2,1)} %grad_ref.1) | copy-start | bytes 1966084
  5.7 10.9 %collective-permute-start = (bf16[32,112,128]{2,1,0:T(8,128)(2,1)S(1)}, bf16[32,112,128]{2,1,0:T(8,128)(2,1)S(1)}, u32[]{:S(2)}, u32[]{:S(2)}) collective-permute-start(bf16[32,112,128]{2,1,0:T(8,128)(2,1)S(1)} %get-tuple-element.9), channel_id=1, source_target_pairs={{0,8},{8,0},{1,9},{9,1},{2,10},{10,2},{3,11},{11,3},{4,12},{12,4},... | collective-permute-start | bytes 2752520 | tf_op jit(solution)/shard_map/ppermute | solution.py:179
  16.6 34.8 %copy-start.1 = (bf16[512,512]{1,0:T(8,128)(2,1)S(1)}, bf16[512,512]{1,0:T(8,128)(2,1)}, u32[]{:S(2)}) copy-start(bf16[512,512]{1,0:T(8,128)(2,1)} %constant.6.clone.table_ref) | copy-start | bytes 1572868
  16.6 34.8 %copy-start.2 = (f32[28,512]{1,0:T(8,128)S(1)}, f32[28,512]{1,0:T(8,128)}, u32[]{:S(2)}) copy-start(f32[28,512]{1,0:T(8,128)} %master_ref.1) | copy-start | bytes 172036
  16.6 34.8 %copy-start.3 = (f32[28,512]{1,0:T(8,128)S(1)}, f32[28,512]{1,0:T(8,128)}, u32[]{:S(2)}) copy-start(f32[28,512]{1,0:T(8,128)} %one_ref.1) | copy-start | bytes 172036
  16.6 34.8 %copy-start.4 = (f32[28,512]{1,0:T(8,128)S(1)}, f32[28,512]{1,0:T(8,128)}, u32[]{:S(2)}) copy-start(f32[28,512]{1,0:T(8,128)} %two_ref.1) | copy-start | bytes 172036
  16.6 34.8 %copy-start.5 = (s32[512]{0:T(512)S(1)}, s32[512]{0:T(512)}, u32[]{:S(2)}) copy-start(s32[512]{0:T(512)} %param.13) | copy-start | bytes 6148

commit v4 on v3

--- a/solution.py
+++ b/solution.py
@@ -54,12 +54,10 @@
 def partial_kernel(
     rows,
     cuts,
-    step_ref,
     hidden_ref,
     grad_ref,
     keep_ref,
     send_ref,
-    powers_ref,
     units,
     grad,
     held,
@@ -91,13 +89,9 @@
             keep_ref[done] = jnp.where(first, lower, upper).astype(jnp.bfloat16)
             send_ref[done] = jnp.where(first, upper, lower).astype(jnp.bfloat16)
             done += 1
-    shape = powers_ref.shape[1:]
-    steps_done = jnp.broadcast_to(step_ref[...], shape).astype(jnp.float32)
-    for i, base in enumerate((0.9, 0.95)):
-        powers_ref[i] = jnp.power(jnp.full(shape, base, jnp.float32), steps_done)
-
-
-def partials(step_count, hidden, out_grad, rows, chips):
+
+
+def partials(hidden, out_grad, rows, chips):
     tokens, units = hidden.shape
     columns = out_grad.shape[1]
     high = rows * columns // LANES
@@ -108,9 +102,9 @@
     block = jax.ShapeDtypeStruct((chips, high, LANES), jnp.bfloat16)
     return pl.pallas_call(
         functools.partial(partial_kernel, rows, cuts),
-        out_shape=[block, block, jax.ShapeDtypeStruct((2, 8, LANES), jnp.float32)],
-        in_specs=[vmem, hbm, hbm],
-        out_specs=[vmem, vmem, vmem],
+        out_shape=[block, block],
+        in_specs=[hbm, hbm],
+        out_specs=[vmem, vmem],
         scratch_shapes=[
             pltpu.VMEM((tokens, units), jnp.bfloat16),
             pltpu.VMEM((tokens, columns), jnp.bfloat16),
@@ -119,7 +113,7 @@
         ],
         compiler_params=pltpu.CompilerParams(vmem_limit_bytes=PARTIAL_VMEM),
         name="partials",
-    )(step_count, hidden, out_grad)
+    )(hidden, out_grad)
 
 
 def update_kernel(
@@ -175,8 +169,13 @@
     rows = master.shape[0]
     swap = [(0, 1), (1, 0)]
     table = jnp.asarray(signs_table(columns), jnp.bfloat16)
-    keep, send, powers = partials(step_count[None, :], hidden, out_grad, rows, zh * y)
+    keep, send = partials(hidden, out_grad, rows, zh * y)
     met = lax.ppermute(send, "c", swap)
+    steps_done = jnp.broadcast_to(step_count.astype(jnp.float32), (8, LANES))
+    powers = jnp.stack(
+        [jnp.power(jnp.full((8, LANES), base, jnp.float32), steps_done) for base in (0.9, 0.95)]
+    )
+    keep, powers = lax.optimization_barrier((keep, powers))
     pair = (keep.astype(jnp.float32) + met.astype(jnp.float32)).astype(jnp.bfloat16)
     got = lax.all_to_all(pair, ("zh", "y"), 0, 0)
     update, own = update_step(

time: 92.2 us -> 91.4 us (level)
  no operation moved by 1% of the time
where the time goes in v4:
time: 91.4 us; the launch traced here: 91.1 us
  blocking collectives  71.8 us (79%)
  starting transfers between devices  8.79 us (10%)
  Pallas kernels  4.54 us (5%)
  other arithmetic  2.03 us (2%)
  between operations  1.44 us (2%)
  local copies, waits for them, and re-layouts  1.29 us (1%)
  waiting for transfers between devices  1.24 us (1%)
    all_to_all x1, blocking collectives, local(): got = lax.all_to_all(pair, ('zh', 'y'), 0, 0)  34.5 us
    all_gather x1, blocking collectives, local(): whole = lax.all_gather(by_z, ('y', 'c'), axis=1, tiled=True)  26.8 us
    all_to_all x1, blocking collectives, local(): lax.all_to_all(jnp.broadcast_to(own[None], (zh, rows, columns)), 'zh', 0, 0)  10.5 us
    ppermute x1, starting transfers between devices, local(): met = lax.ppermute(send, 'c', swap)  8.79 us
    pallas_call x1, Pallas kernels, partials(): pl.pallas_call(functools.partial(partial_kernel, rows, cuts), out_shape=[...  3.31 us
  transfers between devices with their start and end apart: 1, of which 1 were waited for; matrix products, arithmetic and copies ran while one was open for 0% of the time, Pallas kernels for 0%

profile of v4, /device:TPU:1, one launch (start us, length us, event | category | flops | bytes accessed | tf_op | source)
XLA Modules:
  0.0 91.1 jit_solution(12519591949023110303)
XLA Ops:
  0.6 0.0 copy-start
  0.6 1.1 %copy-done = bf16[640,512]{1,0:T(8,128)(2,1)S(1)} copy-done((bf16[640,512]{1,0:T(8,128)(2,1)S(1)}, bf16[640,512]{1,0:T(8,128)(2,1)}, u32[]{:S(2)}) %copy-start) | copy-done | bytes 655384
  1.7 3.3 %partials.1 = (bf16[32,112,128]{2,1,0:T(8,128)(2,1)S(1)}, bf16[32,112,128]{2,1,0:T(8,128)(2,1)S(1)}) custom-call(bf16[640,1792]{1,0:T(8,128)(2,1)} %hidden_ref.1, bf16[640,512]{1,0:T(8,128)(2,1)S(1)} %copy-done), custom_call_target="tpu_custom_call" | custom-call | tf_op jit(solution)/shard_map/partials/pallas_call | solution.py:103
  5.0 8.8 %collective-permute-start = (bf16[32,112,128]{2,1,0:T(8,128)(2,1)S(1)}, bf16[32,112,128]{2,1,0:T(8,128)(2,1)S(1)}, u32[]{:S(2)}, u32[]{:S(2)}) collective-permute-start(bf16[32,112,128]{2,1,0:T(8,128)(2,1)S(1)} %get-tuple-element.11), channel_id=1, source_target_pairs={{0,8},{8,0},{1,9},{9,1},{2,10},{10,2},{3,11},{11,3},{4,12},{12,4},... | collective-permute-start | bytes 2752520 | tf_op jit(solution)/shard_map/ppermute | solution.py:173
  14.6 0.1 stack.8.powers_ref
  14.6 0.0 copy-start.1
  14.6 0.0 copy-start.2
  14.6 0.0 copy-start.3
  14.6 0.0 copy-start.4
  14.7 0.0 copy-start.5
  14.7 1.2 %collective-permute-done = bf16[32,112,128]{2,1,0:T(8,128)(2,1)S(1)} collective-permute-done((bf16[32,112,128]{2,1,0:T(8,128)(2,1)S(1)}, bf16[32,112,128]{2,1,0:T(8,128)(2,1)S(1)}, u32[]{:S(2)}, u32[]{:S(2)}) %collective-permute-start) | collective-permute-done | bytes 917536 | tf_op jit(solution)/shard_map/ppermute | solution.py:173
  15.9 0.2 add_convert_fusion
  16.2 34.5 %all_to_all.10.got_ref = bf16[32,112,128]{2,1,0:T(8,128)(2,1)S(1)} all-to-all(bf16[32,112,128]{2,1,0:T(8,128)(2,1)S(1)} %add_convert_fusion), channel_id=1, replica_groups=mesh['zh'=4,'y'=8,'c'=2,'zl'=2,'x'=4] {'zh','y'}, dimensions={0} | all-to-all | bytes 1835008 | tf_op jit(solution)/shard_map/all_to_all | solution.py:180
  50.6 0.0 copy-done.1
  50.6 0.0 copy-done.2
  50.6 0.0 copy-done.3
  50.6 0.0 copy-done.4
  50.6 0.0 copy-done.5
  50.6 1.2 %update_step.1 = (f32[28,512]{1,0:T(8,128)}, f32[28,512]{1,0:T(8,128)S(1)}) custom-call(f32[2,8,128]{2,1,0:T(8,128)S(1)} %stack.8.powers_ref, bf16[32,112,128]{2,1,0:T(8,128)(2,1)S(1)} %all_to_all.10.got_ref, f32[28,512]{1,0:T(8,128)S(1)} %copy-done.2, f32[28,512]{1,0:T(8,128)S(1)} %copy-done.3, f32[28,512]{1,0:T(8,128)S(1)} %copy-done.4, ...), custom_call_target="tpu_custom_call" | custom-call | tf_op jit(solution)/shard_map/update_step/pallas_call | solution.py:156
  51.9 10.5 %all_to_all.11 = f16[4,28,512]{2,1,0:T(8,128)(2,1)S(1)} all-to-all(f16[4,28,512]{2,1,0:T(8,128)(2,1)S(1)} %broadcast_in_dim.5), channel_id=1, replica_groups=mesh['zh'=4,'y'=8,'c'=2,'zl'=2,'x'=4] {'zh'}, dimensions={0} | all-to-all | bytes 229376 | tf_op jit(solution)/shard_map/all_to_all | solution.py:192
  62.4 0.1 copy.11
  62.5 26.8 %all-gather.1 = f16[4,448,512]{2,0,1:T(4,128)(2,1)S(1)} all-gather(f16[4,28,512]{2,0,1:T(4,128)(2,1)S(1)} %copy.11), channel_id=1, replica_groups=mesh['zh'=4,'y'=8,'c'=2,'zl'=2,'x'=4] {'y','c'}, dimensions={1}, use_global_device_ids=true | all-gather | bytes 1949696 | tf_op jit(solution)/shard_map/all_gather | solution.py:193
  89.4 1.8 %multiply_convert_fusion = bf16[4,448,512]{2,1,0:T(8,128)(2,1)} fusion(f16[4,448,512]{2,0,1:T(4,128)(2,1)S(1)} %all-gather.1), kind=kLoop, calls=%fused_computation | loop fusion | flops 2752512 | bytes 3670016 | tf_op jit(solution)/shard_map/convert_element_type | solution.py:194
  (3 shorter events, 0.0 us)
Async XLA Ops:
  0.6 1.1 %copy-start = (bf16[640,512]{1,0:T(8,128)(2,1)S(1)}, bf16[640,512]{1,0:T(8,128)(2,1)}, u32[]{:S(2)}) copy-start(bf16[640,512]{1,0:T(8,128)(2,1)} %grad_ref.1) | copy-start | bytes 1966084
  5.0 10.9 %collective-permute-start = (bf16[32,112,128]{2,1,0:T(8,128)(2,1)S(1)}, bf16[32,112,128]{2,1,0:T(8,128)(2,1)S(1)}, u32[]{:S(2)}, u32[]{:S(2)}) collective-permute-start(bf16[32,112,128]{2,1,0:T(8,128)(2,1)S(1)} %get-tuple-element.11), channel_id=1, source_target_pairs={{0,8},{8,0},{1,9},{9,1},{2,10},{10,2},{3,11},{11,3},{4,12},{12,4},... | collective-permute-start | bytes 2752520 | tf_op jit(solution)/shard_map/ppermute | solution.py:173
  14.6 36.0 %copy-start.1 = (bf16[512,512]{1,0:T(8,128)(2,1)S(1)}, bf16[512,512]{1,0:T(8,128)(2,1)}, u32[]{:S(2)}) copy-start(bf16[512,512]{1,0:T(8,128)(2,1)} %constant.12.clone.table_ref) | copy-start | bytes 1572868
  14.6 36.0 %copy-start.2 = (f32[28,512]{1,0:T(8,128)S(1)}, f32[28,512]{1,0:T(8,128)}, u32[]{:S(2)}) copy-start(f32[28,512]{1,0:T(8,128)} %master_ref.1) | copy-start | bytes 172036
  14.6 36.0 %copy-start.3 = (f32[28,512]{1,0:T(8,128)S(1)}, f32[28,512]{1,0:T(8,128)}, u32[]{:S(2)}) copy-start(f32[28,512]{1,0:T(8,128)} %one_ref.1) | copy-start | bytes 172036
  14.6 36.0 %copy-start.4 = (f32[28,512]{1,0:T(8,128)S(1)}, f32[28,512]{1,0:T(8,128)}, u32[]{:S(2)}) copy-start(f32[28,512]{1,0:T(8,128)} %two_ref.1) | copy-start | bytes 172036
  14.7 36.0 %copy-start.5 = (s32[512]{0:T(512)S(1)}, s32[512]{0:T(512)}, u32[]{:S(2)}) copy-start(s32[512]{0:T(512)} %param.13) | copy-start | bytes 6148

commit v5 on v4

--- a/solution.py
+++ b/solution.py
@@ -38,6 +38,9 @@
 
 
 def exact_dot(value, table):
+    half = table.shape[0]
+    left, right = value[:, :half], value[:, half:]
+    value = jnp.concatenate([left + right, left - right], axis=0)
     rows = value.shape[0]
     high = value.astype(jnp.bfloat16)
     rest = value - high.astype(jnp.float32)
@@ -48,11 +51,13 @@
         table,
         preferred_element_type=jnp.float32,
     )
-    return parts[:rows] + (parts[rows : 2 * rows] + parts[2 * rows :])
+    total = parts[:rows] + (parts[rows : 2 * rows] + parts[2 * rows :])
+    return jnp.concatenate([total[: rows // 2], total[rows // 2 :]], axis=1)
 
 
 def partial_kernel(
     rows,
+    orders,
     cuts,
     hidden_ref,
     grad_ref,
@@ -86,12 +91,15 @@
         while 2 * rows * (done + 1) <= stop:
             both = held[2 * rows * done : 2 * rows * (done + 1), :]
             lower, upper = pack(both[:rows]), pack(both[rows:])
-            keep_ref[done] = jnp.where(first, lower, upper).astype(jnp.bfloat16)
-            send_ref[done] = jnp.where(first, upper, lower).astype(jnp.bfloat16)
+            by_core = [order[done] for order in orders]
+            mine = jnp.where(first, by_core[0], by_core[1])
+            other = jnp.where(first, by_core[1], by_core[0])
+            keep_ref[mine] = jnp.where(first, lower, upper).astype(jnp.bfloat16)
+            send_ref[other] = jnp.where(first, upper, lower).astype(jnp.bfloat16)
             done += 1
 
 
-def partials(hidden, out_grad, rows, chips):
+def partials(hidden, out_grad, rows, chips, orders):
     tokens, units = hidden.shape
     columns = out_grad.shape[1]
     high = rows * columns // LANES
@@ -101,7 +109,7 @@
     hbm = pl.BlockSpec(memory_space=pltpu.HBM)
     block = jax.ShapeDtypeStruct((chips, high, LANES), jnp.bfloat16)
     return pl.pallas_call(
-        functools.partial(partial_kernel, rows, cuts),
+        functools.partial(partial_kernel, rows, orders, cuts),
         out_shape=[block, block],
         in_specs=[hbm, hbm],
         out_specs=[vmem, vmem],
@@ -163,13 +171,14 @@
     )(powers, got, master, moment_one, moment_two, flips, table)
 
 
-def local(hidden, out_grad, master, moment_one, moment_two, sign_flips, step_count):
+def local(orders, groups, hidden, out_grad, master, moment_one, moment_two, sign_flips, step_count):
     columns = out_grad.shape[1]
     zh, y, c = (lax.axis_size(a) for a in DP)
     rows = master.shape[0]
+    chips = zh * y
     swap = [(0, 1), (1, 0)]
-    table = jnp.asarray(signs_table(columns), jnp.bfloat16)
-    keep, send = partials(hidden, out_grad, rows, zh * y)
+    table = jnp.asarray(signs_table(columns // 2), jnp.bfloat16)
+    keep, send = partials(hidden, out_grad, rows, chips, orders)
     met = lax.ppermute(send, "c", swap)
     steps_done = jnp.broadcast_to(step_count.astype(jnp.float32), (8, LANES))
     powers = jnp.stack(
@@ -177,7 +186,11 @@
     )
     keep, powers = lax.optimization_barrier((keep, powers))
     pair = (keep.astype(jnp.float32) + met.astype(jnp.float32)).astype(jnp.bfloat16)
-    got = lax.all_to_all(pair, ("zh", "y"), 0, 0)
+    near_size = len(groups[0][0])
+    pair = pair.reshape((near_size, chips // near_size) + pair.shape[1:])
+    near = lax.all_to_all(pair, DP + MP, 0, 0, axis_index_groups=groups[0])
+    near = jnp.sum(near.astype(jnp.float32), axis=0).astype(jnp.bfloat16)
+    got = lax.all_to_all(near, DP + MP, 0, 0, axis_index_groups=groups[1])
     update, own = update_step(
         powers,
         got,
@@ -195,11 +208,29 @@
     return (weights.reshape(-1, columns), update)
 
 
+def two_stages(sizes):
+    zh, y, c, zl, x = sizes
+    numbers = np.arange(np.prod(sizes)).reshape(sizes)
+    split = numbers.reshape(zh, 4, y // 4, c, zl, x)
+    near0 = np.moveaxis(split[:, :, :, 0], 1, -1).reshape(-1, 4)
+    far0 = np.moveaxis(split[:, :, :, 0], (0, 2), (-2, -1)).reshape(-1, 8)
+    near1 = np.moveaxis(numbers[:, :, 1], 0, -1).reshape(-1, 4)
+    far1 = np.moveaxis(numbers[:, :, 1], 1, -1).reshape(-1, 8)
+    groups = (
+        np.concatenate([near0, near1]).tolist(),
+        np.concatenate([far0, far1]).tolist(),
+    )
+    chips = np.arange(zh * y)
+    order0 = chips.reshape(4, zh, y // 4).transpose(1, 0, 2).reshape(-1)
+    return (order0.tolist(), chips.tolist()), groups
+
+
 def solution(mesh):
-    inner = Mesh(mesh.devices.reshape(4, 8, 2, 2, 4), DP + MP)
+    sizes = (4, 8, 2, 2, 4)
+    inner = Mesh(mesh.devices.reshape(sizes), DP + MP)
     owner = P(MP + DP, None)
     return jax.shard_map(
-        local,
+        functools.partial(local, *two_stages(sizes)),
         mesh=inner,
         in_specs=(P(DP, MP), P(DP, None), owner, owner, owner, P(), P()),
         out_specs=(P(MP, None), owner),

time: 91.4 us -> 90.8 us (level)
    all_gather x1, blocking collectives: 26.8 us -> 24.8 us  [local(): whole = lax.all_gather(by_z, ('y', 'c'), axis=1, tiled=True)]
    all_to_all x1 -> x2, blocking collectives: 34.5 us -> 35.9 us  [the longest x1 20.6 us: local(): near = lax.all_to_all(pair, DP + MP, 0, 0, axis_index_groups=groups[0])]
where the time goes in v5:
time: 90.8 us; the launch traced here: 90.5 us
  blocking collectives  71.1 us (78%)
  starting transfers between devices  8.79 us (10%)
  Pallas kernels  4.36 us (5%)
  other arithmetic  2.19 us (2%)
  between operations  1.47 us (2%)
  local copies, waits for them, and re-layouts  1.3 us (1%)
  waiting for transfers between devices  1.27 us (1%)
    all_gather x1, blocking collectives, local(): whole = lax.all_gather(by_z, ('y', 'c'), axis=1, tiled=True)  24.8 us
    all_to_all x1, blocking collectives, local(): near = lax.all_to_all(pair, DP + MP, 0, 0, axis_index_groups=groups[0])  20.6 us
    all_to_all x1, blocking collectives, local(): got = lax.all_to_all(near, DP + MP, 0, 0, axis_index_groups=groups[1])  15.3 us
    all_to_all x1, blocking collectives, local(): lax.all_to_all(jnp.broadcast_to(own[None], (zh, rows, columns)), 'zh', 0, 0)  10.4 us
    ppermute x1, starting transfers between devices, local(): met = lax.ppermute(send, 'c', swap)  8.79 us
    pallas_call x1, Pallas kernels, partials(): pl.pallas_call(functools.partial(partial_kernel, rows, orders, cuts), out...  3.31 us
  transfers between devices with their start and end apart: 1, of which 1 were waited for; matrix products, arithmetic and copies ran while one was open for 0% of the time, Pallas kernels for 0%

profile of v5, /device:TPU:1, one launch (start us, length us, event | category | flops | bytes accessed | tf_op | source)
XLA Modules:
  0.0 90.5 jit_solution(6751934939020084617)
XLA Ops:
  0.6 0.0 copy-start
  0.6 1.1 %copy-done = bf16[640,512]{1,0:T(8,128)(2,1)S(1)} copy-done((bf16[640,512]{1,0:T(8,128)(2,1)S(1)}, bf16[640,512]{1,0:T(8,128)(2,1)}, u32[]{:S(2)}) %copy-start) | copy-done | bytes 655384
  1.7 3.3 %partials.1 = (bf16[32,112,128]{2,1,0:T(8,128)(2,1)S(1)}, bf16[32,112,128]{2,1,0:T(8,128)(2,1)S(1)}) custom-call(bf16[640,1792]{1,0:T(8,128)(2,1)} %hidden_ref.1, bf16[640,512]{1,0:T(8,128)(2,1)S(1)} %copy-done), custom_call_target="tpu_custom_call" | custom-call | tf_op jit(solution)/shard_map/partials/pallas_call | solution.py:111
  5.0 8.8 %collective-permute-start = (bf16[32,112,128]{2,1,0:T(8,128)(2,1)S(1)}, bf16[32,112,128]{2,1,0:T(8,128)(2,1)S(1)}, u32[]{:S(2)}, u32[]{:S(2)}) collective-permute-start(bf16[32,112,128]{2,1,0:T(8,128)(2,1)S(1)} %get-tuple-element.11), channel_id=1, source_target_pairs={{0,8},{8,0},{1,9},{9,1},{2,10},{10,2},{3,11},{11,3},{4,12},{12,4},... | collective-permute-start | bytes 2752520 | tf_op jit(solution)/shard_map/ppermute | solution.py:182
  14.6 0.1 stack.8.powers_ref
  14.6 1.3 %collective-permute-done = bf16[32,112,128]{2,1,0:T(8,128)(2,1)S(1)} collective-permute-done((bf16[32,112,128]{2,1,0:T(8,128)(2,1)S(1)}, bf16[32,112,128]{2,1,0:T(8,128)(2,1)S(1)}, u32[]{:S(2)}, u32[]{:S(2)}) %collective-permute-start) | collective-permute-done | bytes 917536 | tf_op jit(solution)/shard_map/ppermute | solution.py:182
  15.9 0.2 add_convert_fusion
  16.2 0.0 copy-start.1
  16.2 0.0 copy-start.2
  16.2 0.0 copy-start.3
  16.2 0.0 copy-start.4
  16.2 0.0 copy-start.5
  16.2 20.6 %all_to_all.15 = bf16[4,8,112,128]{3,2,1,0:T(8,128)(2,1)S(1)} all-to-all(bf16[4,8,112,128]{3,2,1,0:T(8,128)(2,1)S(1)} %bitcast.5), channel_id=1, replica_groups={{0,32,64,96},{1,33,65,97},{2,34,66,98},{3,35,67,99},{4,36,68,100},{5,37..., dimensions={0} | all-to-all | bytes 1835008 | tf_op jit(solution)/shard_map/all_to_all | solution.py:191
  36.8 0.2 reduce_sum.12
  36.9 15.3 %all_to_all.16.got_ref = bf16[8,112,128]{2,1,0:T(8,128)(2,1)S(1)} all-to-all(bf16[8,112,128]{2,1,0:T(8,128)(2,1)S(1)} %reduce_sum.12), channel_id=1, replica_groups={{0,16,128,144,256,272,384,400},{1,17,129,145,257,273,385,401},{2,18,130..., dimensions={0} | all-to-all | bytes 458752 | tf_op jit(solution)/shard_map/all_to_all | solution.py:193
  52.2 0.0 copy-done.1
  52.2 0.0 copy-done.2
  52.2 0.0 copy-done.3
  52.2 0.0 copy-done.4
  52.2 0.0 copy-done.5
  52.3 1.0 %update_step.1 = (f32[28,512]{1,0:T(8,128)}, f32[28,512]{1,0:T(8,128)S(1)}) custom-call(f32[2,8,128]{2,1,0:T(8,128)S(1)} %stack.8.powers_ref, bf16[8,112,128]{2,1,0:T(8,128)(2,1)S(1)} %all_to_all.16.got_ref, f32[28,512]{1,0:T(8,128)S(1)} %copy-done.2, f32[28,512]{1,0:T(8,128)S(1)} %copy-done.3, f32[28,512]{1,0:T(8,128)S(1)} %copy-done.4, ...), custom_call_target="tpu_custom_call" | custom-call | tf_op jit(solution)/shard_map/update_step/pallas_call | solution.py:164
  53.3 10.4 %all_to_all.17 = f16[4,28,512]{2,1,0:T(8,128)(2,1)S(1)} all-to-all(f16[4,28,512]{2,1,0:T(8,128)(2,1)S(1)} %broadcast_in_dim.5), channel_id=1, replica_groups=mesh['zh'=4,'y'=8,'c'=2,'zl'=2,'x'=4] {'zh'}, dimensions={0} | all-to-all | bytes 229376 | tf_op jit(solution)/shard_map/all_to_all | solution.py:205
  63.8 0.1 copy.11
  63.9 24.8 %all-gather.1 = f16[4,448,512]{2,0,1:T(4,128)(2,1)S(1)} all-gather(f16[4,28,512]{2,0,1:T(4,128)(2,1)S(1)} %copy.11), channel_id=1, replica_groups=mesh['zh'=4,'y'=8,'c'=2,'zl'=2,'x'=4] {'y','c'}, dimensions={1}, use_global_device_ids=true | all-gather | bytes 1949696 | tf_op jit(solution)/shard_map/all_gather | solution.py:206
  88.7 1.8 %multiply_convert_fusion = bf16[4,448,512]{2,1,0:T(8,128)(2,1)} fusion(f16[4,448,512]{2,0,1:T(4,128)(2,1)S(1)} %all-gather.1), kind=kLoop, calls=%fused_computation | loop fusion | flops 2752512 | bytes 3670016 | tf_op jit(solution)/shard_map/convert_element_type | solution.py:207
  (3 shorter events, 0.0 us)
Async XLA Ops:
  0.6 1.1 %copy-start = (bf16[640,512]{1,0:T(8,128)(2,1)S(1)}, bf16[640,512]{1,0:T(8,128)(2,1)}, u32[]{:S(2)}) copy-start(bf16[640,512]{1,0:T(8,128)(2,1)} %grad_ref.1) | copy-start | bytes 1966084
  5.0 10.9 %collective-permute-start = (bf16[32,112,128]{2,1,0:T(8,128)(2,1)S(1)}, bf16[32,112,128]{2,1,0:T(8,128)(2,1)S(1)}, u32[]{:S(2)}, u32[]{:S(2)}) collective-permute-start(bf16[32,112,128]{2,1,0:T(8,128)(2,1)S(1)} %get-tuple-element.11), channel_id=1, source_target_pairs={{0,8},{8,0},{1,9},{9,1},{2,10},{10,2},{3,11},{11,3},{4,12},{12,4},... | collective-permute-start | bytes 2752520 | tf_op jit(solution)/shard_map/ppermute | solution.py:182
  16.2 36.1 %copy-start.1 = (bf16[256,256]{1,0:T(8,128)(2,1)S(1)}, bf16[256,256]{1,0:T(8,128)(2,1)}, u32[]{:S(2)}) copy-start(bf16[256,256]{1,0:T(8,128)(2,1)} %constant.15.clone.table_ref) | copy-start | bytes 393220
  16.2 36.1 %copy-start.2 = (f32[28,512]{1,0:T(8,128)S(1)}, f32[28,512]{1,0:T(8,128)}, u32[]{:S(2)}) copy-start(f32[28,512]{1,0:T(8,128)} %master_ref.1) | copy-start | bytes 172036
  16.2 36.1 %copy-start.3 = (f32[28,512]{1,0:T(8,128)S(1)}, f32[28,512]{1,0:T(8,128)}, u32[]{:S(2)}) copy-start(f32[28,512]{1,0:T(8,128)} %one_ref.1) | copy-start | bytes 172036
  16.2 36.1 %copy-start.4 = (f32[28,512]{1,0:T(8,128)S(1)}, f32[28,512]{1,0:T(8,128)}, u32[]{:S(2)}) copy-start(f32[28,512]{1,0:T(8,128)} %two_ref.1) | copy-start | bytes 172036
  16.2 36.1 %copy-start.5 = (s32[512]{0:T(512)S(1)}, s32[512]{0:T(512)}, u32[]{:S(2)}) copy-start(s32[512]{0:T(512)} %param.13) | copy-start | bytes 6148
